TPU v7x, 128 devices: a whole 4x4x4 slice. The times are simulated.
128 devices in a mesh: section: 8 (over x, core), expert: 16 (over y, z).
Axes of the slice: x: 4, y: 4, z: 4, core: 2. Of those that a mesh axis runs over, the one named last changes fastest.
Arguments:
- inputs: bfloat16 [8, 2048, 2048], P('section', 'expert'), may hold values from -6 to 6
- out_grad: bfloat16 [8, 2048, 2048], P('section', 'expert'), may hold values from -6 to 6
- expert_ids: int32 [8, 2048, 8], P('section', 'expert'), may hold values from 0 to 15, all different within a row; in each aligned block of 128 rows (0 to 127, 128 to 255, ..., all dimensions but the last counted through in order) at most 72 rows name the same one
- gate_probs: bfloat16 [8, 2048, 8], P('section', 'expert'), may hold values from 0.049804688 to 0.59765625
- gate_weight: bfloat16 [8, 16, 2048, 768], P('section', 'expert'), may hold values from -0.125 to 0.125
- up_weight: bfloat16 [8, 16, 2048, 768], P('section', 'expert'), may hold values from -0.125 to 0.125
- down_weight: bfloat16 [8, 16, 768, 2048], P('section', 'expert'), may hold values from -0.21875 to 0.21875
Outputs:
- handed_grad: bfloat16 [8, 2048, 2048], P('section', 'expert')
- gate_grad: bfloat16 [8, 2048, 8], P('section', 'expert')
- gate_wgrad: bfloat16 [8, 16, 2048, 768], P('section', 'expert')
- up_wgrad: bfloat16 [8, 16, 2048, 768], P('section', 'expert')
- down_wgrad: bfloat16 [8, 16, 768, 2048], P('section', 'expert')
Inputs may be any that keep to these rules, and one draw needn't show every extreme that they name: `expert_ids`: each row names 8 different experts. Among the rows of one device (aligned blocks of 128 rows) no expert is named by more than 72 rows, a bound that some block reaches.
All inputs are finite; a program needn't handle non-finite values.
Results may differ from a plain program's by a relative error of at most 0.011.
Values may be sent and summed in bfloat16 or wider, within the bound.
No kernel may reach another device: no remote copies, remote signals or barrier semaphores. Data moves between devices by JAX's collectives and lax.ppermute only.
A program may use at most 128 MiB of HBM per device.

v0:
```python
import jax
import jax.numpy as jnp
from jax import lax
from jax.sharding import PartitionSpec as P


def from_behind(block, axis, distance):
    devices = range(lax.axis_size(axis))
    route = [(i - distance, i) for i in devices if i - distance in devices]
    return lax.ppermute(block, axis, route)


def route_tables(expert_ids, experts, capacity):
    columns = jnp.arange(experts, dtype=jnp.int32)
    matches = expert_ids[:, :, None] == columns[None, None, :]
    member = jnp.sum(matches.astype(jnp.int32), axis=1)
    slot_rank = jnp.cumsum(member, axis=0) - member
    slot_index = jnp.arange(capacity, dtype=jnp.int32)
    placed = (member[:, :, None] == 1) & (slot_rank[:, :, None] == slot_index[None, None, :])
    return (matches, placed)


def expert_backward(rows_in, rows_grad, rows_gate, gate_mat, up_mat, down_mat):
    by_cols = (((1,), (1,)), ((), ()))
    by_rows = (((0,), (0,)), ((), ()))
    pre_gate = jnp.dot(rows_in, gate_mat, preferred_element_type=jnp.float32)
    pre_up = jnp.dot(rows_in, up_mat, preferred_element_type=jnp.float32)
    sig_gate = jax.nn.sigmoid(pre_gate)
    active = pre_gate * sig_gate
    hidden = active * pre_up
    down_back = lax.dot_general(rows_grad, down_mat, by_cols, preferred_element_type=jnp.float32)
    slot_grad = jnp.sum(hidden * down_back, axis=1).astype(jnp.bfloat16)
    weight = rows_gate.astype(jnp.float32)[:, None]
    scaled = weight * down_back
    hidden_gated = (weight * hidden).astype(jnp.bfloat16)
    down_wgrad = lax.dot_general(
        hidden_gated, rows_grad, by_rows, preferred_element_type=jnp.float32
    )
    grad_gate = (scaled * pre_up * sig_gate * (1.0 + pre_gate * (1.0 - sig_gate))).astype(
        jnp.bfloat16
    )
    grad_up = (scaled * active).astype(jnp.bfloat16)
    rows_back = (
        lax.dot_general(grad_gate, gate_mat, by_cols, preferred_element_type=jnp.float32)
        + lax.dot_general(grad_up, up_mat, by_cols, preferred_element_type=jnp.float32)
    ).astype(jnp.bfloat16)
    gate_wgrad = lax.dot_general(rows_in, grad_gate, by_rows, preferred_element_type=jnp.float32)
    up_wgrad = lax.dot_general(rows_in, grad_up, by_rows, preferred_element_type=jnp.float32)
    return (
        rows_back,
        slot_grad,
        gate_wgrad.astype(jnp.bfloat16),
        up_wgrad.astype(jnp.bfloat16),
        down_wgrad.astype(jnp.bfloat16),
    )


def local(inputs, out_grad, expert_ids, gate_probs, gate_weight, up_weight, down_weight):
    tokens_in = inputs[0]
    token_grad = out_grad[0]
    local_ids = expert_ids[0]
    gate_values = gate_probs[0]
    width = tokens_in.shape[1]
    tok_count = tokens_in.shape[0]
    route_count = local_ids.shape[1]
    experts = lax.axis_size("expert")
    capacity = min(tok_count, 9 * tok_count * route_count // (8 * experts))
    matches, placed = route_tables(local_ids, experts, capacity)
    gate_table = jnp.sum(
        jnp.where(matches, gate_values[:, :, None].astype(jnp.float32), 0.0), axis=1
    )
    gate_mat = gate_weight[0, 0]
    up_mat = up_weight[0, 0]
    down_mat = down_weight[0, 0]
    placed_half = placed.astype(jnp.bfloat16)
    placed_wide = placed.astype(jnp.float32)
    send_in = jnp.einsum(
        "tec,td->ecd", placed_half, tokens_in, preferred_element_type=jnp.float32
    ).astype(jnp.bfloat16)
    send_grad = jnp.einsum(
        "tec,td->ecd", placed_half, token_grad, preferred_element_type=jnp.float32
    ).astype(jnp.bfloat16)
    send_gate = jnp.einsum("tec,te->ec", placed_wide, gate_table).astype(jnp.bfloat16)
    rows_in, rows_grad, rows_gate = (
        lax.all_to_all(send_in, "expert", split_axis=0, concat_axis=0, tiled=True),
        lax.all_to_all(send_grad, "expert", split_axis=0, concat_axis=0, tiled=True),
        lax.all_to_all(send_gate, "expert", split_axis=0, concat_axis=0, tiled=True),
    )
    rows_back, slot_grad, gate_wgrad, up_wgrad, down_wgrad = expert_backward(
        rows_in.reshape(experts * capacity, width),
        rows_grad.reshape(experts * capacity, width),
        rows_gate.reshape(experts * capacity),
        gate_mat,
        up_mat,
        down_mat,
    )
    back_rows, back_gate = (
        lax.all_to_all(
            rows_back.reshape(experts, capacity, width),
            "expert",
            split_axis=0,
            concat_axis=0,
            tiled=True,
        ),
        lax.all_to_all(
            slot_grad.reshape(experts, capacity), "expert", split_axis=0, concat_axis=0, tiled=True
        ),
    )
    moe_sum = jnp.einsum("tec,ecd->td", placed_half, back_rows, preferred_element_type=jnp.float32)
    back_wide = lax.optimization_barrier(back_gate).astype(jnp.float32)
    token_table = jnp.einsum("tec,ec->te", placed_wide, back_wide)
    gate_grad = jnp.sum(jnp.where(matches, token_table[:, None, :], 0.0), axis=2).astype(
        jnp.bfloat16
    )
    moe_part = moe_sum.astype(jnp.bfloat16)
    summed = (token_grad.astype(jnp.float32) + moe_part.astype(jnp.float32)).astype(jnp.bfloat16)
    handed_grad = from_behind(summed, "section", -1)
    return (
        handed_grad[None],
        gate_grad[None],
        gate_wgrad[None, None],
        up_wgrad[None, None],
        down_wgrad[None, None],
    )


def solution(mesh):
    placed = (
        P("section", "expert", None),
        P("section", "expert", None),
        P("section", "expert", None),
        P("section", "expert", None),
        P("section", "expert", None, None),
        P("section", "expert", None, None),
        P("section", "expert", None, None),
    )
    return jax.shard_map(
        local,
        mesh=mesh,
        in_specs=placed,
        out_specs=(
            P("section", "expert", None),
            P("section", "expert", None),
            P("section", "expert", None, None),
            P("section", "expert", None, None),
            P("section", "expert", None, None),
        ),
        check_vma=False,
    )
```

profile of v0, /device:TPU:1, one launch (start us, length us, event | category | flops | bytes accessed | tf_op | source)
XLA Modules:
  0.0 282.1 jit_solution(2504077514433599242)
XLA Ops:
  0.6 0.9 convert_reduce_fusion
  1.9 4.6 %convolution_convert_fusion = bf16[16,72,2048]{2,1,0:T(8,128)(2,1)} fusion(bf16[1,128,2048]{2,1,0:T(8,128)(2,1)} %param.7, s32[128,16]{0,1:T(8,128)S(1)} %copy.33, pred[128,16]{0,1:T(8,128)(4,1)S(1)} %broadcast_compare_fusion), kind=kOutput, calls=%fused_computation.1 | convolution fusion | flops 606633984 | bytes 5253120 | tf_op jit(solution)/shard_map/tec,td->ecd/dot_general | solution.py:77
  6.5 8.6 %all-to-all-start.2 = ((bf16[16,72,2048]{2,1,0:T(8,128)(2,1)}), bf16[16,72,2048]{2,1,0:T(8,128)(2,1)}, u32[]{:S(2)}, u32[]{:S(2)}) async-start(bf16[16,72,2048]{2,1,0:T(8,128)(2,1)} %convolution_convert_fusion), calls=%async_computation.2 | async-start | bytes 9437184 | tf_op jit(solution)/shard_map/all_to_all | solution.py:85
  15.1 4.7 %convolution_convert_fusion.1 = bf16[16,72,2048]{2,1,0:T(8,128)(2,1)} fusion(bf16[1,128,2048]{2,1,0:T(8,128)(2,1)} %param.8, s32[128,16]{0,1:T(8,128)S(1)} %copy.33, pred[128,16]{0,1:T(8,128)(4,1)S(1)} %broadcast_compare_fusion), kind=kOutput, calls=%fused_computation.2 | convolution fusion | flops 606633984 | bytes 5253120 | tf_op jit(solution)/shard_map/tec,td->ecd/dot_general | solution.py:80
  19.8 67.1 %all-to-all-done.2 = bf16[16,72,2048]{2,1,0:T(8,128)(2,1)} async-done(((bf16[16,72,2048]{2,1,0:T(8,128)(2,1)}), bf16[16,72,2048]{2,1,0:T(8,128)(2,1)}, u32[]{:S(2)}, u32[]{:S(2)}) %all-to-all-start.2) | async-done | bytes 4718624 | tf_op jit(solution)/shard_map/all_to_all | solution.py:85
  86.9 9.2 %all-to-all-start.1 = ((bf16[16,72,2048]{2,1,0:T(8,128)(2,1)}), bf16[16,72,2048]{2,1,0:T(8,128)(2,1)}, u32[]{:S(2)}, u32[]{:S(2)}) async-start(bf16[16,72,2048]{2,1,0:T(8,128)(2,1)} %convolution_convert_fusion.1), calls=%async_computation.1 | async-start | bytes 9437184 | tf_op jit(solution)/shard_map/all_to_all | solution.py:86
  96.2 8.6 %fusion.3 = f32[1152,768]{0,1:T(8,128)} fusion(bf16[1152,2048]{1,0:T(8,128)(2,1)} %bitcast.13, bf16[1,1,2048,768]{3,2,1,0:T(8,128)(2,1)S(1)} %copy-done), kind=kOutput, calls=%fused_computation.14 | convolution fusion | flops 3623878656 | bytes 11403264 | tf_op jit(solution)/shard_map/dot_general | solution.py:26
  104.8 8.5 %fusion.6 = f32[1152,768]{0,1:T(8,128)} fusion(bf16[1152,2048]{1,0:T(8,128)(2,1)} %bitcast.13, bf16[1,1,2048,768]{3,2,1,0:T(8,128)(2,1)S(1)} %copy-done.11), kind=kOutput, calls=%fused_computation.17 | convolution fusion | flops 3623878656 | bytes 11403264 | tf_op jit(solution)/shard_map/dot_general | solution.py:27
  113.3 39.0 %all-to-all-done.1 = bf16[16,72,2048]{2,1,0:T(8,128)(2,1)} async-done(((bf16[16,72,2048]{2,1,0:T(8,128)(2,1)}), bf16[16,72,2048]{2,1,0:T(8,128)(2,1)}, u32[]{:S(2)}, u32[]{:S(2)}) %all-to-all-start.1) | async-done | bytes 4718624 | tf_op jit(solution)/shard_map/all_to_all | solution.py:86
  152.3 11.8 %multiply_reduce_fusion = (bf16[1152]{0:T(1024)(128)(2,1)S(1)}, f32[1152,768]{0,1:T(8,128)}) fusion(f32[1152,768]{0,1:T(8,128)} %fusion.6, f32[1152,768]{0,1:T(8,128)} %fusion.3, bf16[1152,2048]{1,0:T(8,128)(2,1)} %bitcast.9, bf16[1,1,768,2048]{3,2,1,0:T(8,128)(2,1)} %param.13), kind=kOutput, calls=%fused_computation.4 | convolution fusion | flops 3630070784 | bytes 18483456 | tf_op jit(solution)/shard_map/dot_general | solution.py:31
  164.7 6.1 %all-to-all-start.4 = ((bf16[16,1,72]{2,1,0:T(2,128)(2,1)}), bf16[16,1,72]{2,1,0:T(2,128)(2,1)S(1)}, u32[]{:S(2)}, u32[]{:S(2)}) async-start(bf16[16,1,72]{2,1,0:T(2,128)(2,1)} %convert_element_type.121), calls=%async_computation.4 | async-start | bytes 16384 | tf_op jit(solution)/shard_map/all_to_all | solution.py:105
  170.8 6.3 %all-to-all-done.4 = bf16[16,1,72]{2,1,0:T(2,128)(2,1)S(1)} async-done(((bf16[16,1,72]{2,1,0:T(2,128)(2,1)}), bf16[16,1,72]{2,1,0:T(2,128)(2,1)S(1)}, u32[]{:S(2)}, u32[]{:S(2)}) %all-to-all-start.4) | async-done | bytes 2336 | tf_op jit(solution)/shard_map/all_to_all | solution.py:105
  178.3 9.1 %all_to_all.33 = bf16[16,1,72]{2,1,0:T(2,128)(2,1)S(1)} all-to-all(bf16[16,1,72]{2,1,0:T(2,128)(2,1)S(1)} %copy.34), channel_id=1, replica_groups=mesh['section'=8,'expert'=16] {'expert'}, dimensions={0} | all-to-all | bytes 4608 | tf_op jit(solution)/shard_map/all_to_all | solution.py:87
  187.5 5.0 %multiply_convert_fusion.1 = (bf16[1152,768]{0,1:T(8,128)(2,1)S(1)}, bf16[1152,768]{0,1:T(8,128)(2,1)S(1)}) fusion(f32[1152,768]{0,1:T(8,128)} %get-tuple-element.10, f32[1152]{0:T(1024)S(1)} %reshape.81, f32[1152,768]{0,1:T(8,128)} %fusion.3, f32[1152,768]{0,1:T(8,128)} %fusion.6), kind=kLoop, calls=%fused_computation.5 | loop fusion | flops 12386304 | bytes 14160384 | tf_op jit(solution)/shard_map/convert_element_type | solution.py:42
  192.5 3.9 %fusion.1 = f32[1152,2048]{1,0:T(8,128)S(1)} fusion(bf16[1152,768]{0,1:T(8,128)(2,1)S(1)} %get-tuple-element.8, bf16[1,1,2048,768]{3,2,1,0:T(8,128)(2,1)S(1)} %copy-done), kind=kOutput, calls=%fused_computation.12 | convolution fusion | flops 3623878656 | bytes 14352384 | tf_op jit(solution)/shard_map/dot_general | solution.py:44
  196.5 5.7 %add_convert_fusion = bf16[1152,2048]{1,0:T(8,128)(2,1)} fusion(f32[1152,2048]{1,0:T(8,128)S(1)} %fusion.1, bf16[1152,768]{0,1:T(8,128)(2,1)S(1)} %get-tuple-element.7, bf16[1,1,2048,768]{3,2,1,0:T(8,128)(2,1)S(1)} %copy-done.12), kind=kOutput, calls=%fused_computation | convolution fusion | flops 3628597248 | bytes 19070976 | tf_op jit(solution)/shard_map/dot_general | solution.py:45
  202.2 4.9 %all-to-all-start.3 = ((bf16[16,72,2048]{2,1,0:T(8,128)(2,1)}), bf16[16,72,2048]{2,1,0:T(8,128)(2,1)}, u32[]{:S(2)}, u32[]{:S(2)}) async-start(bf16[16,72,2048]{2,1,0:T(8,128)(2,1)} %bitcast.78), calls=%async_computation.3 | async-start | bytes 9437184 | tf_op jit(solution)/shard_map/all_to_all | solution.py:98
  207.2 8.2 %fusion.11 = bf16[1,1,2048,768]{3,2,1,0:T(8,128)(2,1)} fusion(bf16[1152,2048]{1,0:T(8,128)(2,1)} %bitcast.13, bf16[1152,768]{0,1:T(8,128)(2,1)S(1)} %copy-done.8), kind=kOutput, calls=%fused_computation.22 | convolution fusion | flops 3625451520 | bytes 9633792 | tf_op jit(solution)/shard_map/dot_general | solution.py:48
  215.5 8.1 %fusion.12 = bf16[1,1,768,2048]{3,2,1,0:T(8,128)(2,1)} fusion(bf16[1152,2048]{1,0:T(8,128)(2,1)} %bitcast.9, f32[1152]{0:T(1024)S(1)} %reshape.81, f32[1152,768]{0,1:T(8,128)S(1)} %copy-done.3, f32[1152,768]{0,1:T(8,128)S(1)} %copy-done.2), kind=kOutput, calls=%fused_computation.23 | convolution fusion | flops 3631644672 | bytes 14946816 | tf_op jit(solution)/shard_map/dot_general | solution.py:36
  223.6 41.6 %all-to-all-done.3 = bf16[16,72,2048]{2,1,0:T(8,128)(2,1)} async-done(((bf16[16,72,2048]{2,1,0:T(8,128)(2,1)}), bf16[16,72,2048]{2,1,0:T(8,128)(2,1)}, u32[]{:S(2)}, u32[]{:S(2)}) %all-to-all-start.3) | async-done | bytes 4718624 | tf_op jit(solution)/shard_map/all_to_all | solution.py:98
  265.2 3.4 %fusion.16 = bf16[128,2048]{1,0:T(8,128)(2,1)S(1)} fusion(bf16[16,72,2048]{2,1,0:T(8,128)(2,1)} %all-to-all-done.3, bf16[1,128,2048]{2,1,0:T(8,128)(2,1)S(1)} %copy-done.4, s32[128,16]{0,1:T(8,128)S(1)} %copy.33, pred[128,16]{0,1:T(8,128)(4,1)S(1)} %broadcast_compare_fusion), kind=kOutput, calls=%fused_computation.28 | convolution fusion | flops 605585408 | bytes 5777408 | tf_op jit(solution)/shard_map/tec,ecd->td/dot_general | solution.py:109
  268.6 4.4 %collective-permute-start = (bf16[128,2048]{1,0:T(8,128)(2,1)S(1)}, bf16[128,2048]{1,0:T(8,128)(2,1)S(1)}, u32[]{:S(2)}, u32[]{:S(2)}) collective-permute-start(bf16[128,2048]{1,0:T(8,128)(2,1)S(1)} %fusion.16), channel_id=1, source_target_pairs={{16,0},{32,16},{48,32},{64,48},{80,64},{96,80},{112,96},{17,1},{33... | collective-permute-start | bytes 1572872 | tf_op jit(solution)/shard_map/ppermute | solution.py:10
  273.0 8.3 %fusion.10 = bf16[1,1,2048,768]{3,2,1,0:T(8,128)(2,1)} fusion(bf16[1152,2048]{1,0:T(8,128)(2,1)} %bitcast.13, bf16[1152,768]{0,1:T(8,128)(2,1)S(1)} %copy-done.6), kind=kOutput, calls=%fused_computation.21 | convolution fusion | flops 3625451520 | bytes 9633792 | tf_op jit(solution)/shard_map/dot_general | solution.py:47
  281.3 0.8 copy.46
  (42 shorter events, 2.3 us)
Async XLA Ops:
  0.6 95.5 %copy-start = (bf16[1,1,2048,768]{3,2,1,0:T(8,128)(2,1)S(1)}, bf16[1,1,2048,768]{3,2,1,0:T(8,128)(2,1)}, u32[]{:S(2)}) copy-start(bf16[1,1,2048,768]{3,2,1,0:T(8,128)(2,1)} %param.11) | copy-start | bytes 9437188
  6.5 80.4 %all-to-all-start.2 = ((bf16[16,72,2048]{2,1,0:T(8,128)(2,1)}), bf16[16,72,2048]{2,1,0:T(8,128)(2,1)}, u32[]{:S(2)}, u32[]{:S(2)}) async-start(bf16[16,72,2048]{2,1,0:T(8,128)(2,1)} %convolution_convert_fusion), calls=%async_computation.2 | async-start | bytes 9437184 | tf_op jit(solution)/shard_map/all_to_all | solution.py:85
  86.9 65.4 %all-to-all-start.1 = ((bf16[16,72,2048]{2,1,0:T(8,128)(2,1)}), bf16[16,72,2048]{2,1,0:T(8,128)(2,1)}, u32[]{:S(2)}, u32[]{:S(2)}) async-start(bf16[16,72,2048]{2,1,0:T(8,128)(2,1)} %convolution_convert_fusion.1), calls=%async_computation.1 | async-start | bytes 9437184 | tf_op jit(solution)/shard_map/all_to_all | solution.py:86
  96.1 8.6 %copy-start.11 = (bf16[1,1,2048,768]{3,2,1,0:T(8,128)(2,1)S(1)}, bf16[1,1,2048,768]{3,2,1,0:T(8,128)(2,1)}, u32[]{:S(2)}) copy-start(bf16[1,1,2048,768]{3,2,1,0:T(8,128)(2,1)} %param.12) | copy-start | bytes 9437188
  152.3 18.5 %copy-start.10 = (bf16[1,128,8]{1,2,0:T(8,128)(2,1)S(1)}, bf16[1,128,8]{1,2,0:T(8,128)(2,1)}, u32[]{:S(2)}) copy-start(bf16[1,128,8]{1,2,0:T(8,128)(2,1)} %param.10) | copy-start | bytes 6148
  152.3 25.1 %copy-start.9 = (s32[1,128,8]{1,2,0:T(8,128)S(1)}, s32[1,128,8]{1,2,0:T(8,128)}, u32[]{:S(2)}) copy-start(s32[1,128,8]{1,2,0:T(8,128)} %param.9) | copy-start | bytes 12292
  164.7 12.4 %all-to-all-start.4 = ((bf16[16,1,72]{2,1,0:T(2,128)(2,1)}), bf16[16,1,72]{2,1,0:T(2,128)(2,1)S(1)}, u32[]{:S(2)}, u32[]{:S(2)}) async-start(bf16[16,1,72]{2,1,0:T(2,128)(2,1)} %convert_element_type.121), calls=%async_computation.4 | async-start | bytes 16384 | tf_op jit(solution)/shard_map/all_to_all | solution.py:105
  192.5 4.0 %copy-start.5 = (bf16[1152,768]{0,1:T(8,128)(2,1)}, bf16[1152,768]{0,1:T(8,128)(2,1)S(1)}, u32[]{:S(2)}) copy-start(bf16[1152,768]{0,1:T(8,128)(2,1)S(1)} %get-tuple-element.8) | copy-start | bytes 5308420
  192.5 4.0 %copy-start.7 = (bf16[1152,768]{0,1:T(8,128)(2,1)}, bf16[1152,768]{0,1:T(8,128)(2,1)S(1)}, u32[]{:S(2)}) copy-start(bf16[1152,768]{0,1:T(8,128)(2,1)S(1)} %get-tuple-element.7) | copy-start | bytes 5308420
  192.5 4.0 %copy-start.12 = (bf16[1,1,2048,768]{3,2,1,0:T(8,128)(2,1)S(1)}, bf16[1,1,2048,768]{3,2,1,0:T(8,128)(2,1)}, u32[]{:S(2)}) copy-start(bf16[1,1,2048,768]{3,2,1,0:T(8,128)(2,1)} %param.12) | copy-start | bytes 9437188
  202.2 5.0 %copy-start.8 = (bf16[1152,768]{0,1:T(8,128)(2,1)S(1)}, bf16[1152,768]{0,1:T(8,128)(2,1)}, u32[]{:S(2)}) copy-start(bf16[1152,768]{0,1:T(8,128)(2,1)} %copy-done.7) | copy-start | bytes 5308420
  202.2 63.0 %all-to-all-start.3 = ((bf16[16,72,2048]{2,1,0:T(8,128)(2,1)}), bf16[16,72,2048]{2,1,0:T(8,128)(2,1)}, u32[]{:S(2)}, u32[]{:S(2)}) async-start(bf16[16,72,2048]{2,1,0:T(8,128)(2,1)} %bitcast.78), calls=%async_computation.3 | async-start | bytes 9437184 | tf_op jit(solution)/shard_map/all_to_all | solution.py:98
  207.2 8.3 %copy-start.2 = (f32[1152,768]{0,1:T(8,128)S(1)}, f32[1152,768]{0,1:T(8,128)}, u32[]{:S(2)}) copy-start(f32[1152,768]{0,1:T(8,128)} %fusion.3) | copy-start | bytes 10616836
  207.2 8.3 %copy-start.3 = (f32[1152,768]{0,1:T(8,128)S(1)}, f32[1152,768]{0,1:T(8,128)}, u32[]{:S(2)}) copy-start(f32[1152,768]{0,1:T(8,128)} %fusion.6) | copy-start | bytes 10616836
  215.5 49.7 %copy-start.4 = (bf16[1,128,2048]{2,1,0:T(8,128)(2,1)S(1)}, bf16[1,128,2048]{2,1,0:T(8,128)(2,1)}, u32[]{:S(2)}) copy-start(bf16[1,128,2048]{2,1,0:T(8,128)(2,1)} %param.8) | copy-start | bytes 1572868
  265.2 7.8 %copy-start.6 = (bf16[1152,768]{0,1:T(8,128)(2,1)S(1)}, bf16[1152,768]{0,1:T(8,128)(2,1)}, u32[]{:S(2)}) copy-start(bf16[1152,768]{0,1:T(8,128)(2,1)} %copy-done.5) | copy-start | bytes 5308420
  268.6 12.8 %collective-permute-start = (bf16[128,2048]{1,0:T(8,128)(2,1)S(1)}, bf16[128,2048]{1,0:T(8,128)(2,1)S(1)}, u32[]{:S(2)}, u32[]{:S(2)}) collective-permute-start(bf16[128,2048]{1,0:T(8,128)(2,1)S(1)} %fusion.16), channel_id=1, source_target_pairs={{16,0},{32,16},{48,32},{64,48},{80,64},{96,80},{112,96},{17,1},{33... | collective-permute-start | bytes 1572872 | tf_op jit(solution)/shard_map/ppermute | solution.py:10
  273.0 9.1 %copy-start.1 = (bf16[1,1,2048,768]{3,2,1,0:T(8,128)(2,1)S(1)}, bf16[1,1,2048,768]{3,2,1,0:T(8,128)(2,1)}, u32[]{:S(2)}) copy-start(bf16[1,1,2048,768]{3,2,1,0:T(8,128)(2,1)} %param.11) | copy-start | bytes 9437188
where the time goes:
time: 283 us; the launch traced here: 282 us
  waiting for transfers between devices  154 us (54%)
  matrix products  76.3 us (27%)
  starting transfers between devices  33.3 us (12%)
  blocking collectives  9.12 us (3%)
  other arithmetic  6.68 us (2%)
    all_to_all x1, waiting for transfers between devices, local(): lax.all_to_all(send_in, 'expert', split_axis=0, concat_axis=0, tiled=True)  67.1 us
    all_to_all x1, waiting for transfers between devices, local(): lax.all_to_all(rows_back.reshape(experts, capacity, width), 'expert', spl...  41.6 us
    all_to_all x1, waiting for transfers between devices, local(): lax.all_to_all(send_grad, 'expert', split_axis=0, concat_axis=0, tiled=True)  39 us
    dot_general x1, matrix products, expert_backward(): lax.dot_general(rows_grad, down_mat, by_cols, preferred_element_type=jnp....  11.8 us
    all_to_all x1, starting transfers between devices, local(): lax.all_to_all(send_grad, 'expert', split_axis=0, concat_axis=0, tiled=True)  9.24 us
    all_to_all x1, blocking collectives, local(): lax.all_to_all(send_gate, 'expert', split_axis=0, concat_axis=0, tiled=True)  9.12 us
    all_to_all x1, starting transfers between devices, local(): lax.all_to_all(send_in, 'expert', split_axis=0, concat_axis=0, tiled=True)  8.64 us
    dot_general x1, matrix products, expert_backward(): pre_gate = jnp.dot(rows_in, gate_mat, preferred_element_type=jnp.float32)  8.6 us
  transfers between devices with their start and end apart: 5, of which 4 were waited for; matrix products, arithmetic and copies ran while one was open for 16% of the time, Pallas kernels for 0%

commit v1 on v0

v1 whole, which is shorter than its diff:
```python
import functools

import jax
import jax.numpy as jnp
from jax import lax
from jax.experimental import pallas as pl
from jax.experimental.pallas import tpu as pltpu
from jax.sharding import PartitionSpec as P

SIDE = 4
CAP = 72
GROUP = SIDE * CAP
META = 8
BF16 = jnp.bfloat16
F32 = jnp.float32
VMEM = pl.BlockSpec(memory_space=pltpu.VMEM)
SMEM = pl.BlockSpec(memory_space=pltpu.SMEM)
BY_COLS = (((1,), (1,)), ((), ()))
BY_ROWS = (((0,), (0,)), ((), ()))


def shift(block, down, over):
    route = []
    for row in range(SIDE):
        for col in range(SIDE):
            to = (row + down) % SIDE * SIDE + (col + over) % SIDE
            route.append((row * SIDE + col, to))
    return lax.ppermute(block, "expert", route)


def params(mib=56):
    return pltpu.CompilerParams(vmem_limit_bytes=mib * 1024 * 1024)


def cost(flops, nbytes):
    return pl.CostEstimate(flops=flops, bytes_accessed=nbytes, transcendentals=0)


def slots(id_blocks, experts):
    hits = []
    for ids, expert in zip(id_blocks, experts):
        hits.append(jnp.sum(jnp.where(ids == expert, 1.0, 0.0), axis=0, keepdims=True))
    hit = jnp.concatenate(hits, axis=0)
    pad = -len(hits) % 8
    if pad:
        hit = jnp.concatenate([hit, jnp.zeros((pad, hit.shape[1]), F32)], axis=0)
    tokens = hit.shape[1]
    earlier = lax.broadcasted_iota(jnp.int32, (tokens, tokens), 0) < lax.broadcasted_iota(
        jnp.int32, (tokens, tokens), 1
    )
    before = jnp.where(earlier, 1.0, 0.0).astype(BF16)
    rank = jnp.dot(hit.astype(BF16), before, preferred_element_type=F32)
    slot = jnp.where(hit > 0.5, rank, -1.0)
    return [slot[i : i + 1] for i in range(len(hits))]


def one_hot(slot, rows, first=0):
    row = lax.broadcasted_iota(jnp.int32, (rows, slot.shape[1]), 0)
    wanted = jnp.where(slot >= 0.0, slot + first, -1.0).astype(jnp.int32)
    return jnp.where(row == wanted, 1.0, 0.0)


def as_float(expert):
    return expert.astype(F32)


def pack_kernel(x_ref, g_ref, ids_ref, gates_ref, a_ref, b_ref):
    tokens, width = x_ref.shape
    meta = jnp.concatenate(
        [
            ids_ref[...].astype(F32),
            gates_ref[...].astype(F32),
            jnp.zeros((META, width - 2 * tokens), F32),
        ],
        axis=1,
    ).astype(BF16)
    a_ref[0:tokens] = x_ref[...]
    a_ref[tokens : tokens + META] = meta
    b_ref[0:tokens] = g_ref[...]
    b_ref[tokens : tokens + META] = meta


def pack(x, g, ids, gates):
    tokens, width = x.shape
    out = jax.ShapeDtypeStruct((tokens + META, width), BF16)
    return pl.pallas_call(
        pack_kernel,
        out_shape=(out, out),
        in_specs=[VMEM] * 4,
        out_specs=(VMEM, VMEM),
        compiler_params=params(16),
        cost_estimate=cost(0, 4 * tokens * width * 2),
    )(x, g, ids, gates)


def select_kernel(tokens, who_ref, *refs):
    a_refs, b_refs, (a_out, b_out) = refs[:4], refs[4:8], refs[8:]
    width = a_out.shape[1]
    ids = [r[tokens : tokens + META, 0:tokens].astype(F32) for r in (*a_refs, *b_refs)]
    experts = [as_float(who_ref[0])] * 4 + [as_float(who_ref[1])] * 4
    slot = slots(ids, experts)
    for refs_of, out, part in ((a_refs, a_out, slot[:4]), (b_refs, b_out, slot[4:])):
        picks = [one_hot(s, CAP).astype(BF16) for s in part]
        for left in range(0, width, 512):
            rows = [
                jnp.dot(p, r[0:tokens, left : left + 512], preferred_element_type=F32)
                for p, r in zip(picks, refs_of)
            ]
            out[0:GROUP, left : left + 512] = jnp.concatenate(rows, axis=0).astype(BF16)
    meta = [r[tokens : tokens + META, 0 : 2 * tokens].astype(F32) for r in a_refs]
    meta.append(jnp.zeros((META, width - 8 * tokens), F32))
    a_out[GROUP : GROUP + META] = jnp.concatenate(meta, axis=1).astype(BF16)


def select(who, a, b, tokens):
    width = a[0].shape[1]
    return pl.pallas_call(
        functools.partial(select_kernel, tokens),
        out_shape=(
            jax.ShapeDtypeStruct((GROUP + META, width), BF16),
            jax.ShapeDtypeStruct((GROUP, width), BF16),
        ),
        in_specs=[SMEM] + [VMEM] * 8,
        out_specs=(VMEM, VMEM),
        compiler_params=params(24),
        cost_estimate=cost(4 * GROUP * tokens * width, 7_000_000),
    )(who, *a, *b)


def sources(a_refs, tokens, expert):
    ids, gates = [], []
    for ref in a_refs:
        for near in range(SIDE):
            left = 2 * tokens * near
            block = ref[GROUP : GROUP + META, left : left + 2 * tokens].astype(F32)
            ids.append(block[:, 0:tokens])
            gates.append(block[:, tokens : 2 * tokens])
    slot = slots(ids, [expert] * len(ids))
    gate = [
        jnp.sum(jnp.where(i == expert, v, 0.0), axis=0, keepdims=True) for i, v in zip(ids, gates)
    ]
    return slot, gate


def expert_kernel(tokens, who_ref, *refs):
    a_refs, b_refs, (wg, wu, wd) = refs[:4], refs[4:8], refs[8:11]
    gg_out, gu_out, hg_out = refs[11:14]
    first_out, second_out = refs[14:18], refs[18:22]
    pg, pu, db, total, gate, slot_sum = refs[22:]
    step, last = pl.program_id(0), pl.num_programs(0) - 1
    half = first_out[0].shape[1]

    @pl.when(step == 0)
    def _():
        slot, value = sources(a_refs, tokens, as_float(who_ref[0]))
        for j in range(16):
            column = jnp.sum(one_hot(slot[j], CAP) * value[j], axis=1, keepdims=True)
            gate[j * CAP : (j + 1) * CAP] = column
        slot_sum[...] = jnp.zeros_like(slot_sum)

    for k in range(SIDE):
        at = slice(k * GROUP, (k + 1) * GROUP)
        rows = a_refs[k][0:GROUP]
        pg[at] = jnp.dot(rows, wg[...], preferred_element_type=F32)
        pu[at] = jnp.dot(rows, wu[...], preferred_element_type=F32)
        db[at] = lax.dot_general(b_refs[k][...], wd[...], BY_COLS, preferred_element_type=F32)

    def block(j, carry):
        here = pl.ds(pl.multiple_of(j * CAP, 8), CAP)
        there = pl.ds(pl.multiple_of((j % SIDE) * GROUP + (j // SIDE) * CAP, 8), CAP)
        pre_gate, pre_up, down_back = pg[here], pu[here], db[there]
        weight = gate[here]
        sig = jax.nn.sigmoid(pre_gate)
        active = pre_gate * sig
        hidden = active * pre_up
        slot_sum[here] += jnp.sum(hidden * down_back, axis=1, keepdims=True)
        scaled = weight * down_back
        pg[here] = scaled * pre_up * sig * (1.0 + pre_gate * (1.0 - sig))
        pu[here] = scaled * active
        db[there] = weight * hidden
        return carry

    lax.fori_loop(0, 16, block, 0)
    hg_out[...] = db[...].astype(BF16)
    for k in range(SIDE):
        at = slice(k * GROUP, (k + 1) * GROUP)
        grad_gate, grad_up = pg[at].astype(BF16), pu[at].astype(BF16)
        gg_out[at] = grad_gate
        gu_out[at] = grad_up
        for left in range(0, 2 * half, 512):
            cols = slice(left, left + 512)
            back = lax.dot_general(
                grad_gate, wg[cols], BY_COLS, preferred_element_type=F32
            ) + lax.dot_general(grad_up, wu[cols], BY_COLS, preferred_element_type=F32)

            @pl.when(step == 0)
            def _():
                total[at, cols] = back

            @pl.when(step > 0)
            def _():
                total[at, cols] += back

    @pl.when(step == last)
    def _():
        slot, _ = sources(a_refs, tokens, as_float(who_ref[0]))
        for k in range(SIDE):
            first_out[k][0:GROUP] = total[k * GROUP : (k + 1) * GROUP, 0:half].astype(BF16)
            lines = []
            for near in range(SIDE):
                j = k * SIDE + near
                value = slot_sum[j * CAP : (j + 1) * CAP].astype(BF16).astype(F32)
                lines.append(
                    jnp.sum(one_hot(slot[j], CAP) * value, axis=0, keepdims=True)
                )
            lines.append(jnp.zeros((META - SIDE, tokens), F32))
            table = jnp.concatenate(lines, axis=0)
            table = jnp.concatenate([table, jnp.zeros((META, half - tokens), F32)], axis=1)
            first_out[k][GROUP : GROUP + META] = table.astype(BF16)
            rows = [
                total[m * GROUP + k * CAP : m * GROUP + (k + 1) * CAP, half : 2 * half]
                for m in range(SIDE)
            ]
            second_out[k][...] = jnp.concatenate(rows, axis=0).astype(BF16)


def expert(who, a, b, wg, wu, wd, tokens):
    width, hidden = wg.shape
    tile = 256
    rows, half = SIDE * GROUP, width // 2
    whole = lambda n, m: pl.BlockSpec((n, m), lambda f: (0, 0), pipeline_mode=pl.Buffered(1))
    column = lambda n: pl.BlockSpec((n, tile), lambda f: (0, f))
    fixed = lambda n, m: pl.BlockSpec((n, m), lambda f: (0, 0))
    return pl.pallas_call(
        functools.partial(expert_kernel, tokens),
        grid=(hidden // tile,),
        out_shape=(
            [jax.ShapeDtypeStruct((rows, hidden), BF16)] * 3
            + [jax.ShapeDtypeStruct((GROUP + META, half), BF16)] * SIDE
            + [jax.ShapeDtypeStruct((GROUP, half), BF16)] * SIDE
        ),
        in_specs=(
            [SMEM]
            + [whole(GROUP + META, width)] * SIDE
            + [whole(GROUP, width)] * SIDE
            + [column(width), column(width), pl.BlockSpec((tile, width), lambda f: (f, 0))]
        ),
        out_specs=(
            [column(rows)] * 3
            + [fixed(GROUP + META, half)] * SIDE
            + [fixed(GROUP, half)] * SIDE
        ),
        scratch_shapes=[pltpu.VMEM((rows, tile), F32)] * 3
        + [pltpu.VMEM((rows, width), F32)]
        + [pltpu.VMEM((rows, 1), F32)] * 2,
        compiler_params=params(60),
        cost_estimate=cost(10 * rows * width * hidden, 32_000_000),
    )(who, *a, *b, wg, wu, wd)


def wgrad_kernel(*refs):
    a_refs, b_refs, (gg, gu, hg) = refs[:4], refs[4:8], refs[8:11]
    gate_out, up_out, down_out = refs[11:]
    a = jnp.concatenate([r[0:GROUP] for r in a_refs], axis=0)
    gate_out[...] = lax.dot_general(a, gg[...], BY_ROWS, preferred_element_type=F32).astype(BF16)
    up_out[...] = lax.dot_general(a, gu[...], BY_ROWS, preferred_element_type=F32).astype(BF16)
    b = jnp.concatenate([r[...] for r in b_refs], axis=0)
    down_out[...] = lax.dot_general(hg[...], b, BY_ROWS, preferred_element_type=F32).astype(BF16)


def wgrads(a, b, gg, gu, hg):
    rows, hidden = gg.shape
    width = a[0].shape[1]
    tile = 256
    whole = pl.BlockSpec((rows, hidden), lambda d: (0, 0), pipeline_mode=pl.Buffered(1))
    return pl.pallas_call(
        wgrad_kernel,
        grid=(width // tile,),
        out_shape=(
            jax.ShapeDtypeStruct((width, hidden), BF16),
            jax.ShapeDtypeStruct((width, hidden), BF16),
            jax.ShapeDtypeStruct((hidden, width), BF16),
        ),
        in_specs=[pl.BlockSpec((GROUP + META, tile), lambda d: (0, d))] * SIDE
        + [pl.BlockSpec((GROUP, tile), lambda d: (0, d))] * SIDE
        + [whole] * 3,
        out_specs=(
            pl.BlockSpec((tile, hidden), lambda d: (d, 0)),
            pl.BlockSpec((tile, hidden), lambda d: (d, 0)),
            pl.BlockSpec((hidden, tile), lambda d: (0, d)),
        ),
        compiler_params=params(40),
        cost_estimate=cost(6 * rows * width * hidden, 24_000_000),
    )(*a, *b, gg, gu, hg)


def gather_kernel(tokens, tables, who_ref, *refs):
    id_refs, back_refs, outs = refs[:4], refs[4:8], refs[8:]
    half = back_refs[0].shape[1]
    ids = [r[tokens : tokens + META, 0:tokens].astype(F32) for r in id_refs]
    pairs = [(near, far) for near in range(SIDE) for far in range(SIDE)]
    slot = slots([ids[n] for n, _ in pairs], [as_float(who_ref[f]) for _, f in pairs])
    for near in range(SIDE):
        places = []
        for far in range(SIDE):
            spread = one_hot(slot[near * SIDE + far], GROUP, near * CAP)
            places.append(spread.T.astype(BF16))
        for left in range(0, half, 512):
            cols = slice(left, left + 512)
            part = jnp.dot(places[0], back_refs[0][0:GROUP, cols], preferred_element_type=F32)
            for far in range(1, SIDE):
                part += jnp.dot(
                    places[far], back_refs[far][0:GROUP, cols], preferred_element_type=F32
                )
            outs[near][0:tokens, cols] = part.astype(BF16)
        if tables:
            lines = [
                r[GROUP : GROUP + META, 0:tokens].astype(F32)[near : near + 1] for r in back_refs
            ]
            lines.append(jnp.zeros((META - SIDE, tokens), F32))
            table = jnp.concatenate(lines, axis=0)
            table = jnp.concatenate([table, jnp.zeros((META, half - tokens), F32)], axis=1)
            outs[near][tokens : tokens + META] = table.astype(BF16)


def gather(who, blocks, back, tokens, tables):
    half = back[0].shape[1]
    rows = tokens + META if tables else tokens
    return pl.pallas_call(
        functools.partial(gather_kernel, tokens, tables),
        out_shape=[jax.ShapeDtypeStruct((rows, half), BF16)] * SIDE,
        in_specs=[SMEM] + [VMEM] * 8,
        out_specs=[VMEM] * SIDE,
        compiler_params=params(24),
        cost_estimate=cost(32 * tokens * GROUP * half, 6_000_000),
    )(who, *blocks, *back)


def finish_kernel(tokens, who_ref, g_ref, ids_ref, *refs):
    firsts, seconds, (out, gate_out) = refs[:4], refs[4:8], refs[8:]
    half = firsts[0].shape[1]
    for parts, left in ((firsts, 0), (seconds, half)):
        cols = slice(left, left + half)
        moe = parts[0][0:tokens].astype(F32)
        for part in parts[1:]:
            moe += part[0:tokens].astype(F32)
        moe = moe.astype(BF16).astype(F32)
        out[:, cols] = (g_ref[:, cols].astype(F32) + moe).astype(BF16)
    ids = ids_ref[...]
    grad = jnp.zeros(ids.shape, F32)
    for near in range(SIDE):
        table = firsts[near][tokens : tokens + META, 0:tokens].astype(F32)
        for far in range(SIDE):
            grad += jnp.where(ids == who_ref[near * SIDE + far], table[far : far + 1], 0.0)
    gate_out[...] = grad.astype(BF16)


def finish(who, g, ids, firsts, seconds):
    tokens, width = g.shape
    return pl.pallas_call(
        functools.partial(finish_kernel, tokens),
        out_shape=(
            jax.ShapeDtypeStruct((tokens, width), BF16),
            jax.ShapeDtypeStruct(ids.shape, BF16),
        ),
        in_specs=[SMEM] + [VMEM] * 10,
        out_specs=(VMEM, VMEM),
        compiler_params=params(16),
        cost_estimate=cost(0, 3_500_000),
    )(who, g, ids, *firsts, *seconds)


def local(inputs, out_grad, expert_ids, gate_probs, gate_weight, up_weight, down_weight):
    x, g = inputs[0], out_grad[0]
    tokens = x.shape[0]
    ids, gates = expert_ids[0].T, gate_probs[0].T
    me = lax.axis_index("expert").astype(jnp.int32)
    row, col = me // SIDE, me % SIDE
    near = jnp.arange(SIDE, dtype=jnp.int32)
    same_row = row * SIDE + (col + near) % SIDE
    same_col = (row + near) % SIDE * SIDE + col
    all_experts = ((row + near[:, None]) % SIDE * SIDE + (col + near[None, :]) % SIDE).reshape(-1)

    a0, b0 = pack(x, g, ids, gates)
    a, b = [a0, None, None, None], [b0, None, None, None]
    for d in (2, 1, 3):
        a[d] = shift(a0, d, 0)
        b[d] = shift(b0, 0, d)

    rows_in, rows_grad = [None] * SIDE, [None] * SIDE
    for d in (2, 1, 3, 0):
        send_a, send_b = select(jnp.stack([same_row[d], same_col[d]]), a, b, tokens)
        rows_in[d] = shift(send_a, 0, d) if d else send_a
        rows_grad[d] = shift(send_b, d, 0) if d else send_b

    made = expert(
        me[None], rows_in, rows_grad, gate_weight[0, 0], up_weight[0, 0], down_weight[0, 0], tokens
    )
    gg, gu, hg = made[:3]
    first, second = list(made[3:7]), list(made[7:11])
    for d in (2, 1, 3):
        first[d] = shift(first[d], 0, -d)
        second[d] = shift(second[d], -d, 0)
    gate_wgrad, up_wgrad, down_wgrad = wgrads(rows_in, rows_grad, gg, gu, hg)

    first = gather(same_row, a, first, tokens, True)
    second = gather(same_col, b, second, tokens, False)
    first, second = list(first), list(second)
    for d in (2, 1, 3):
        first[d] = shift(first[d], -d, 0)
        second[d] = shift(second[d], 0, -d)
    section_grad, gate_grad = finish(all_experts, g, ids, first, second)

    sections = lax.axis_size("section")
    handed = lax.ppermute(section_grad, "section", [(i + 1, i) for i in range(sections - 1)])
    return (
        handed[None],
        gate_grad.T[None],
        gate_wgrad[None, None],
        up_wgrad[None, None],
        down_wgrad[None, None],
    )


def solution(mesh):
    rows, mats = P("section", "expert", None), P("section", "expert", None, None)
    return jax.shard_map(
        local,
        mesh=mesh,
        in_specs=(rows, rows, rows, rows, mats, mats, mats),
        out_specs=(rows, rows, mats, mats, mats),
        check_vma=False,
    )
```

time: 283 us -> 260 us (0.919)
  waiting for transfers between devices: 154 us -> 72.2 us
  Pallas kernels: 0 us -> 80.9 us
  matrix products: 76.3 us -> 0 us
  starting transfers between devices: 33.3 us -> 80.7 us
  local copies, waits for them, and re-layouts: 1.81 us -> 18.2 us
  blocking collectives: 9.12 us -> 0 us
    all_to_all x4 -> x0, waiting for transfers between devices: 154 us -> none  [the longest x1 67.1 us: local(): lax.all_to_all(send_in, 'expert', split_axis=0, concat_axis=0, tiled=True)]
    pallas_call x0 -> x10, Pallas kernels: none -> 80.9 us  [the longest x1 45.7 us: expert(): pl.pallas_call(functools.partial(expert_kernel, tokens), grid=(hidden //...]
    dot_general x13 -> x0, matrix products: 76.3 us -> none  [the longest x1 11.8 us: expert_backward(): lax.dot_general(rows_grad, down_mat, by_cols, preferred_element_type=jnp....]
    ppermute x1 -> x25, starting transfers between devices: 4.43 us -> 80.7 us  [the longest x24 78.1 us: shift(): return lax.ppermute(block, 'expert', route)]
    ppermute x1 -> x25, waiting for transfers between devices: 0.01 us -> 72.2 us  [the longest x24 72.2 us: shift(): return lax.ppermute(block, 'expert', route)]
    all_to_all x4 -> x0, starting transfers between devices: 28.9 us -> none  [the longest x1 9.24 us: local(): lax.all_to_all(send_grad, 'expert', split_axis=0, concat_axis=0, tiled=True)]
    unnamed x28 -> x45, local copies, waits for them, and re-layouts: 0.87 us -> 16.9 us
    all_to_all x1 -> x0, blocking collectives: 9.12 us -> none  [local(): lax.all_to_all(send_gate, 'expert', split_axis=0, concat_axis=0, tiled=True)]
  transfers between devices with their start and end apart: 5 -> 25, of which waited for: 4 -> 11; matrix products, arithmetic and copies ran while one was open for 16% -> 3% of each run, Pallas kernels for 0% -> 12%
where the time goes in v1:
time: 260 us; the launch traced here: 258 us
  Pallas kernels  80.9 us (31%)
  starting transfers between devices  80.7 us (31%)
  waiting for transfers between devices  72.2 us (28%)
  local copies, waits for them, and re-layouts  18.2 us (7%)
  other arithmetic  5.34 us (2%)
    ppermute x24, starting transfers between devices, shift(): return lax.ppermute(block, 'expert', route)  78.1 us
    ppermute x24, waiting for transfers between devices, shift(): return lax.ppermute(block, 'expert', route)  72.2 us
    pallas_call x1, Pallas kernels, expert(): pl.pallas_call(functools.partial(expert_kernel, tokens), grid=(hidden //...  45.7 us
    pallas_call x1, Pallas kernels, wgrads(): pl.pallas_call(wgrad_kernel, grid=(width // tile,), out_shape=(jax.ShapeD...  17.2 us
    unnamed x45, local copies, waits for them, and re-layouts  16.9 us
    pallas_call x2, Pallas kernels, gather(): pl.pallas_call(functools.partial(gather_kernel, tokens, tables), out_shap...  8.17 us
    pallas_call x4, Pallas kernels, select(): pl.pallas_call(functools.partial(select_kernel, tokens), out_shape=(jax.S...  8.12 us
    another operation x2, other arithmetic, local(): send_a, send_b = select(jnp.stack([same_row[d], same_col[d]]), a, b, tokens)  5.22 us
  transfers between devices with their start and end apart: 25, of which 11 were waited for; matrix products, arithmetic and copies ran while one was open for 3% of the time, Pallas kernels for 12%

profile of v1, /device:TPU:1, one launch (start us, length us, event | category | flops | bytes accessed | tf_op | source)
XLA Modules:
  0.0 258.2 jit_solution(11556756875123424198)
XLA Ops:
  6.4 2.6 %collective-permute-start.1 = (bf16[136,2048]{1,0:T(8,128)(2,1)S(1)}, bf16[136,2048]{1,0:T(8,128)(2,1)S(1)}, u32[]{:S(2)}, u32[]{:S(2)}) collective-permute-start(bf16[136,2048]{1,0:T(8,128)(2,1)S(1)} %get-tuple-element.39.refs_0_), channel_id=1, source_target_pairs={{0,8},{1,9},{2,10},{3,11},{4,12},{5,13},{6,14},{7,15},{8,0},{9,1},... | collective-permute-start | bytes 1671176 | tf_op jit(solution)/shard_map/ppermute | solution.py:28
  11.7 3.3 %collective-permute-start.4 = (bf16[136,2048]{1,0:T(8,128)(2,1)S(1)}, bf16[136,2048]{1,0:T(8,128)(2,1)}, u32[]{:S(2)}, u32[]{:S(2)}) collective-permute-start(bf16[136,2048]{1,0:T(8,128)(2,1)S(1)} %get-tuple-element.40.refs_4_.refs_0_), channel_id=1, source_target_pairs={{0,2},{1,3},{2,0},{3,1},{4,6},{5,7},{6,4},{7,5},{8,10},{9,11},{10,... | collective-permute-start | bytes 1671176 | tf_op jit(solution)/shard_map/ppermute | solution.py:28
  15.0 5.0 %collective-permute-done.refs_1_ = bf16[136,2048]{1,0:T(8,128)(2,1)S(1)} collective-permute-done((bf16[136,2048]{1,0:T(8,128)(2,1)S(1)}, bf16[136,2048]{1,0:T(8,128)(2,1)S(1)}, u32[]{:S(2)}, u32[]{:S(2)}) %collective-permute-start) | collective-permute-done | bytes 557088 | tf_op jit(solution)/shard_map/ppermute | solution.py:28
  20.0 3.8 %collective-permute-start.5 = (bf16[136,2048]{1,0:T(8,128)(2,1)S(1)}, bf16[136,2048]{1,0:T(8,128)(2,1)S(1)}, u32[]{:S(2)}, u32[]{:S(2)}) collective-permute-start(bf16[136,2048]{1,0:T(8,128)(2,1)S(1)} %get-tuple-element.40.refs_4_.refs_0_), channel_id=1, source_target_pairs={{0,3},{1,0},{2,1},{3,2},{4,7},{5,4},{6,5},{7,6},{8,11},{9,8},{10,9... | collective-permute-start | bytes 1671176 | tf_op jit(solution)/shard_map/ppermute | solution.py:28
  27.7 5.4 %collective-permute-done.1.refs_2_ = bf16[136,2048]{1,0:T(8,128)(2,1)S(1)} collective-permute-done((bf16[136,2048]{1,0:T(8,128)(2,1)S(1)}, bf16[136,2048]{1,0:T(8,128)(2,1)S(1)}, u32[]{:S(2)}, u32[]{:S(2)}) %collective-permute-start.1) | collective-permute-done | bytes 557088 | tf_op jit(solution)/shard_map/ppermute | solution.py:28
  33.1 5.1 %collective-permute-done.4.refs_6_.refs_2_ = bf16[136,2048]{1,0:T(8,128)(2,1)} collective-permute-done((bf16[136,2048]{1,0:T(8,128)(2,1)S(1)}, bf16[136,2048]{1,0:T(8,128)(2,1)}, u32[]{:S(2)}, u32[]{:S(2)}) %collective-permute-start.4) | collective-permute-done | bytes 557088 | tf_op jit(solution)/shard_map/ppermute | solution.py:28
  43.3 3.2 %collective-permute-start.6 = (bf16[296,2048]{1,0:T(8,128)(2,1)S(1)}, bf16[296,2048]{1,0:T(8,128)(2,1)}, u32[]{:S(2)}, u32[]{:S(2)}) collective-permute-start(bf16[296,2048]{1,0:T(8,128)(2,1)S(1)} %get-tuple-element.42), channel_id=1, source_target_pairs={{0,1},{1,2},{2,3},{3,0},{4,5},{5,6},{6,7},{7,4},{8,9},{9,10},{10,1... | collective-permute-start | bytes 3637256 | tf_op jit(solution)/shard_map/ppermute | solution.py:28
  53.2 18.3 %collective-permute-done.9.refs_5_ = bf16[288,2048]{1,0:T(8,128)(2,1)S(1)} collective-permute-done((bf16[288,2048]{1,0:T(8,128)(2,1)S(1)}, bf16[288,2048]{1,0:T(8,128)(2,1)S(1)}, u32[]{:S(2)}, u32[]{:S(2)}) %collective-permute-start.9) | collective-permute-done | bytes 1179680 | tf_op jit(solution)/shard_map/ppermute | solution.py:28
  76.7 12.1 %collective-permute-done.10.refs_6_ = bf16[288,2048]{1,0:T(8,128)(2,1)S(1)} collective-permute-done((bf16[288,2048]{1,0:T(8,128)(2,1)S(1)}, bf16[288,2048]{1,0:T(8,128)(2,1)S(1)}, u32[]{:S(2)}, u32[]{:S(2)}) %collective-permute-start.10) | collective-permute-done | bytes 1179680 | tf_op jit(solution)/shard_map/ppermute | solution.py:28
  88.8 6.5 %collective-permute-done.11.refs_7_ = bf16[288,2048]{1,0:T(8,128)(2,1)S(1)} collective-permute-done((bf16[288,2048]{1,0:T(8,128)(2,1)S(1)}, bf16[288,2048]{1,0:T(8,128)(2,1)S(1)}, u32[]{:S(2)}, u32[]{:S(2)}) %collective-permute-start.11) | collective-permute-done | bytes 1179680 | tf_op jit(solution)/shard_map/ppermute | solution.py:28
  97.8 2.9 %collective-permute-done.8.refs_3_ = bf16[296,2048]{1,0:T(8,128)(2,1)} collective-permute-done((bf16[296,2048]{1,0:T(8,128)(2,1)S(1)}, bf16[296,2048]{1,0:T(8,128)(2,1)}, u32[]{:S(2)}, u32[]{:S(2)}) %collective-permute-start.8) | collective-permute-done | bytes 1212448 | tf_op jit(solution)/shard_map/ppermute | solution.py:28
  100.8 45.7 %shard_map.115 = (bf16[1152,768]{1,0:T(8,128)(2,1)}, bf16[1152,768]{1,0:T(8,128)(2,1)}, bf16[1152,768]{1,0:T(8,128)(2,1)}, bf16[296,1024]{1,0:T(8,128)(2,1)}, bf...) custom-call(s32[1]{0:T(128)} %bitcast.7.who_ref, ...), custom_call_target="tpu_custom_call" | custom-call | flops 18119393280 | bytes 32000000 | tf_op jit(solution)/shard_map/pallas_call | solution.py:234
  149.0 7.0 %collective-permute-start.19 = (bf16[288,1024]{1,0:T(8,128)(2,1)}, bf16[288,1024]{1,0:T(8,128)(2,1)S(1)}, u32[]{:S(2)}, u32[]{:S(2)}) collective-permute-start(bf16[288,1024]{1,0:T(8,128)(2,1)} %get-tuple-element.59), channel_id=1, source_target_pairs={{0,8},{1,9},{2,10},{3,11},{4,12},{5,13},{6,14},{7,15},{8,0},{9,1},... | collective-permute-start | bytes 1769480 | tf_op jit(solution)/shard_map/ppermute | solution.py:28
  156.0 14.3 %collective-permute-start.12 = (bf16[296,1024]{1,0:T(8,128)(2,1)}, bf16[296,1024]{1,0:T(8,128)(2,1)S(1)}, u32[]{:S(2)}, u32[]{:S(2)}) collective-permute-start(bf16[296,1024]{1,0:T(8,128)(2,1)} %get-tuple-element.50), channel_id=1, source_target_pairs={{0,3},{1,0},{2,1},{3,2},{4,7},{5,4},{6,5},{7,6},{8,11},{9,8},{10,9... | collective-permute-start | bytes 1818632 | tf_op jit(solution)/shard_map/ppermute | solution.py:28
  170.3 3.6 %collective-permute-start.13 = (bf16[296,1024]{1,0:T(8,128)(2,1)}, bf16[296,1024]{1,0:T(8,128)(2,1)S(1)}, u32[]{:S(2)}, u32[]{:S(2)}) collective-permute-start(bf16[296,1024]{1,0:T(8,128)(2,1)} %get-tuple-element.51), channel_id=1, source_target_pairs={{0,2},{1,3},{2,0},{3,1},{4,6},{5,7},{6,4},{7,5},{8,10},{9,11},{10,... | collective-permute-start | bytes 1818632 | tf_op jit(solution)/shard_map/ppermute | solution.py:28
  173.8 8.8 %collective-permute-start.14 = (bf16[296,1024]{1,0:T(8,128)(2,1)}, bf16[296,1024]{1,0:T(8,128)(2,1)S(1)}, u32[]{:S(2)}, u32[]{:S(2)}) collective-permute-start(bf16[296,1024]{1,0:T(8,128)(2,1)} %get-tuple-element.52), channel_id=1, source_target_pairs={{0,1},{1,2},{2,3},{3,0},{4,5},{5,6},{6,7},{7,4},{8,9},{9,10},{10,1... | collective-permute-start | bytes 1818632 | tf_op jit(solution)/shard_map/ppermute | solution.py:28
  183.7 4.4 %shard_map.117 = (bf16[128,1024]{1,0:T(8,128)(2,1)S(1)}, bf16[128,1024]{1,0:T(8,128)(2,1)S(1)}, bf16[128,1024]{1,0:T(8,128)(2,1)}, bf16[128,1024]{1,0:T(8,128)(2,1)}) custom-call(s32[4]{0:T(128)S(1)} %broadcast_add_fusion.2.who_ref, bf16[136,2048]{1,0:T(8,128)(2,1)S(1)} %get-tuple-element.40.refs_4_.refs_0_, ...), custom_call_target="tpu_custom_call" | custom-call | flops 1207959552 | bytes 6000000 | tf_op jit(solution)/shard_map/pallas_call | solution.py:329
  188.1 15.9 %collective-permute-start.21 = (bf16[128,1024]{1,0:T(8,128)(2,1)S(1)}, bf16[128,1024]{1,0:T(8,128)(2,1)S(1)}, u32[]{:S(2)}, u32[]{:S(2)}) collective-permute-start(bf16[128,1024]{1,0:T(8,128)(2,1)S(1)} %get-tuple-element.62), channel_id=1, source_target_pairs={{0,3},{1,0},{2,1},{3,2},{4,7},{5,4},{6,5},{7,6},{8,11},{9,8},{10,9... | collective-permute-start | bytes 786440 | tf_op jit(solution)/shard_map/ppermute | solution.py:28
  204.0 3.6 %collective-permute-start.22 = (bf16[128,1024]{1,0:T(8,128)(2,1)}, bf16[128,1024]{1,0:T(8,128)(2,1)S(1)}, u32[]{:S(2)}, u32[]{:S(2)}) collective-permute-start(bf16[128,1024]{1,0:T(8,128)(2,1)} %get-tuple-element.63), channel_id=1, source_target_pairs={{0,2},{1,3},{2,0},{3,1},{4,6},{5,7},{6,4},{7,5},{8,10},{9,11},{10,... | collective-permute-start | bytes 786440 | tf_op jit(solution)/shard_map/ppermute | solution.py:28
  207.6 3.8 %shard_map.116 = (bf16[136,1024]{1,0:T(8,128)(2,1)S(1)}, bf16[136,1024]{1,0:T(8,128)(2,1)}, bf16[136,1024]{1,0:T(8,128)(2,1)}, bf16[136,1024]{1,0:T(8,128)(2,1)}) custom-call(s32[4]{0:T(128)S(1)} %broadcast_add_fusion.1.who_ref, bf16[136,2048]{1,0:T(8,128)(2,1)S(1)} %get-tuple-element.39.refs_0_, bf16[136,2048]{1,0:T(8,128)(2,1)S(1)} %collective-permute-done.refs_1_, ...), custom_call_target="tpu_custom_call" | custom-call | flops 1207959552 | bytes 6000000 | tf_op jit(solution)/shard_map/pallas_call | solution.py:329
  213.3 6.9 %collective-permute-done.23.refs_7_ = bf16[128,1024]{1,0:T(8,128)(2,1)} collective-permute-done((bf16[128,1024]{1,0:T(8,128)(2,1)}, bf16[128,1024]{1,0:T(8,128)(2,1)}, u32[]{:S(2)}, u32[]{:S(2)}) %collective-permute-start.23) | collective-permute-done | bytes 262176 | tf_op jit(solution)/shard_map/ppermute | solution.py:28
  220.2 7.2 %collective-permute-done.17.refs_3_ = bf16[136,1024]{1,0:T(8,128)(2,1)S(1)} collective-permute-done((bf16[136,1024]{1,0:T(8,128)(2,1)}, bf16[136,1024]{1,0:T(8,128)(2,1)S(1)}, u32[]{:S(2)}, u32[]{:S(2)}) %collective-permute-start.17) | collective-permute-done | bytes 278560 | tf_op jit(solution)/shard_map/ppermute | solution.py:28
  230.8 2.6 %collective-permute-start.24 = (bf16[128,2048]{1,0:T(8,128)(2,1)S(1)}, bf16[128,2048]{1,0:T(8,128)(2,1)S(1)}, u32[]{:S(2)}, u32[]{:S(2)}) collective-permute-start(bf16[128,2048]{1,0:T(8,128)(2,1)S(1)} %get-tuple-element.65), channel_id=1, source_target_pairs={{16,0},{32,16},{48,32},{64,48},{80,64},{96,80},{112,96},{17,1},{33... | collective-permute-start | bytes 1572872 | tf_op jit(solution)/shard_map/ppermute | solution.py:415
  240.2 17.2 %shard_map.119 = (bf16[2048,768]{1,0:T(8,128)(2,1)}, bf16[2048,768]{1,0:T(8,128)(2,1)}, bf16[768,2048]{1,0:T(8,128)(2,1)}) custom-call(bf16[296,2048]{1,0:T(8,128)(2,1)S(1)} %copy-done.11, bf16[296,2048]{1,0:T(8,128)(2,1)} %collective-permute-done.6.refs_1_, bf16[296,2048]{1,0:T(8,128)(2,1)} %collective-permute-done.7.refs_2_, ...), custom_call_target="tpu_custom_call" | custom-call | flops 10871635968 | bytes 24000000 | tf_op jit(solution)/shard_map/pallas_call | solution.py:276
  (90 shorter events, 48.4 us)
Async XLA Ops:
  4.2 15.8 %collective-permute-start = (bf16[136,2048]{1,0:T(8,128)(2,1)S(1)}, bf16[136,2048]{1,0:T(8,128)(2,1)S(1)}, u32[]{:S(2)}, u32[]{:S(2)}) collective-permute-start(bf16[136,2048]{1,0:T(8,128)(2,1)S(1)} %get-tuple-element.39.refs_0_), channel_id=1, source_target_pairs={{0,4},{1,5},{2,6},{3,7},{4,8},{5,9},{6,10},{7,11},{8,12},{9,13},{1... | collective-permute-start | bytes 1671176 | tf_op jit(solution)/shard_map/ppermute | solution.py:28
  6.4 26.7 %collective-permute-start.1 = (bf16[136,2048]{1,0:T(8,128)(2,1)S(1)}, bf16[136,2048]{1,0:T(8,128)(2,1)S(1)}, u32[]{:S(2)}, u32[]{:S(2)}) collective-permute-start(bf16[136,2048]{1,0:T(8,128)(2,1)S(1)} %get-tuple-element.39.refs_0_), channel_id=1, source_target_pairs={{0,8},{1,9},{2,10},{3,11},{4,12},{5,13},{6,14},{7,15},{8,0},{9,1},... | collective-permute-start | bytes 1671176 | tf_op jit(solution)/shard_map/ppermute | solution.py:28
  9.0 24.1 %collective-permute-start.2 = (bf16[136,2048]{1,0:T(8,128)(2,1)S(1)}, bf16[136,2048]{1,0:T(8,128)(2,1)S(1)}, u32[]{:S(2)}, u32[]{:S(2)}) collective-permute-start(bf16[136,2048]{1,0:T(8,128)(2,1)S(1)} %get-tuple-element.39.refs_0_), channel_id=1, source_target_pairs={{0,12},{1,13},{2,14},{3,15},{4,0},{5,1},{6,2},{7,3},{8,4},{9,5},{1... | collective-permute-start | bytes 1671176 | tf_op jit(solution)/shard_map/ppermute | solution.py:28
  10.0 23.0 %collective-permute-start.3 = (bf16[136,2048]{1,0:T(8,128)(2,1)S(1)}, bf16[136,2048]{1,0:T(8,128)(2,1)S(1)}, u32[]{:S(2)}, u32[]{:S(2)}) collective-permute-start(bf16[136,2048]{1,0:T(8,128)(2,1)S(1)} %get-tuple-element.40.refs_4_.refs_0_), channel_id=1, source_target_pairs={{0,1},{1,2},{2,3},{3,0},{4,5},{5,6},{6,7},{7,4},{8,9},{9,10},{10,1... | collective-permute-start | bytes 1671176 | tf_op jit(solution)/shard_map/ppermute | solution.py:28
  11.7 26.5 %collective-permute-start.4 = (bf16[136,2048]{1,0:T(8,128)(2,1)S(1)}, bf16[136,2048]{1,0:T(8,128)(2,1)}, u32[]{:S(2)}, u32[]{:S(2)}) collective-permute-start(bf16[136,2048]{1,0:T(8,128)(2,1)S(1)} %get-tuple-element.40.refs_4_.refs_0_), channel_id=1, source_target_pairs={{0,2},{1,3},{2,0},{3,1},{4,6},{5,7},{6,4},{7,5},{8,10},{9,11},{10,... | collective-permute-start | bytes 1671176 | tf_op jit(solution)/shard_map/ppermute | solution.py:28
  20.0 18.2 %collective-permute-start.5 = (bf16[136,2048]{1,0:T(8,128)(2,1)S(1)}, bf16[136,2048]{1,0:T(8,128)(2,1)S(1)}, u32[]{:S(2)}, u32[]{:S(2)}) collective-permute-start(bf16[136,2048]{1,0:T(8,128)(2,1)S(1)} %get-tuple-element.40.refs_4_.refs_0_), channel_id=1, source_target_pairs={{0,3},{1,0},{2,1},{3,2},{4,7},{5,4},{6,5},{7,6},{8,11},{9,8},{10,9... | collective-permute-start | bytes 1671176 | tf_op jit(solution)/shard_map/ppermute | solution.py:28
  40.2 31.3 %collective-permute-start.9 = (bf16[288,2048]{1,0:T(8,128)(2,1)S(1)}, bf16[288,2048]{1,0:T(8,128)(2,1)S(1)}, u32[]{:S(2)}, u32[]{:S(2)}) collective-permute-start(bf16[288,2048]{1,0:T(8,128)(2,1)S(1)} %get-tuple-element.46), channel_id=1, source_target_pairs={{0,4},{1,5},{2,6},{3,7},{4,8},{5,9},{6,10},{7,11},{8,12},{9,13},{1... | collective-permute-start | bytes 3538952 | tf_op jit(solution)/shard_map/ppermute | solution.py:28
  43.3 52.0 %collective-permute-start.6 = (bf16[296,2048]{1,0:T(8,128)(2,1)S(1)}, bf16[296,2048]{1,0:T(8,128)(2,1)}, u32[]{:S(2)}, u32[]{:S(2)}) collective-permute-start(bf16[296,2048]{1,0:T(8,128)(2,1)S(1)} %get-tuple-element.42), channel_id=1, source_target_pairs={{0,1},{1,2},{2,3},{3,0},{4,5},{5,6},{6,7},{7,4},{8,9},{9,10},{10,1... | collective-permute-start | bytes 3637256 | tf_op jit(solution)/shard_map/ppermute | solution.py:28
  48.5 49.3 %collective-permute-start.7 = (bf16[296,2048]{1,0:T(8,128)(2,1)S(1)}, bf16[296,2048]{1,0:T(8,128)(2,1)}, u32[]{:S(2)}, u32[]{:S(2)}) collective-permute-start(bf16[296,2048]{1,0:T(8,128)(2,1)S(1)} %get-tuple-element.43), channel_id=1, source_target_pairs={{0,2},{1,3},{2,0},{3,1},{4,6},{5,7},{6,4},{7,5},{8,10},{9,11},{10,... | collective-permute-start | bytes 3637256 | tf_op jit(solution)/shard_map/ppermute | solution.py:28
  51.1 49.6 %collective-permute-start.8 = (bf16[296,2048]{1,0:T(8,128)(2,1)S(1)}, bf16[296,2048]{1,0:T(8,128)(2,1)}, u32[]{:S(2)}, u32[]{:S(2)}) collective-permute-start(bf16[296,2048]{1,0:T(8,128)(2,1)S(1)} %get-tuple-element.44), channel_id=1, source_target_pairs={{0,3},{1,0},{2,1},{3,2},{4,7},{5,4},{6,5},{7,6},{8,11},{9,8},{10,9... | collective-permute-start | bytes 3637256 | tf_op jit(solution)/shard_map/ppermute | solution.py:28
  53.1 35.7 %collective-permute-start.10 = (bf16[288,2048]{1,0:T(8,128)(2,1)S(1)}, bf16[288,2048]{1,0:T(8,128)(2,1)S(1)}, u32[]{:S(2)}, u32[]{:S(2)}) collective-permute-start(bf16[288,2048]{1,0:T(8,128)(2,1)S(1)} %get-tuple-element.47), channel_id=1, source_target_pairs={{0,8},{1,9},{2,10},{3,11},{4,12},{5,13},{6,14},{7,15},{8,0},{9,1},... | collective-permute-start | bytes 3538952 | tf_op jit(solution)/shard_map/ppermute | solution.py:28
  71.5 23.7 %collective-permute-start.11 = (bf16[288,2048]{1,0:T(8,128)(2,1)S(1)}, bf16[288,2048]{1,0:T(8,128)(2,1)S(1)}, u32[]{:S(2)}, u32[]{:S(2)}) collective-permute-start(bf16[288,2048]{1,0:T(8,128)(2,1)S(1)} %get-tuple-element.48), channel_id=1, source_target_pairs={{0,12},{1,13},{2,14},{3,15},{4,0},{5,1},{6,2},{7,3},{8,4},{9,5},{1... | collective-permute-start | bytes 3538952 | tf_op jit(solution)/shard_map/ppermute | solution.py:28
  146.4 27.4 %collective-permute-start.18 = (bf16[288,1024]{1,0:T(8,128)(2,1)}, bf16[288,1024]{1,0:T(8,128)(2,1)S(1)}, u32[]{:S(2)}, u32[]{:S(2)}) collective-permute-start(bf16[288,1024]{1,0:T(8,128)(2,1)} %get-tuple-element.58), channel_id=1, source_target_pairs={{0,12},{1,13},{2,14},{3,15},{4,0},{5,1},{6,2},{7,3},{8,4},{9,5},{1... | collective-permute-start | bytes 1769480 | tf_op jit(solution)/shard_map/ppermute | solution.py:28
  149.0 33.6 %collective-permute-start.19 = (bf16[288,1024]{1,0:T(8,128)(2,1)}, bf16[288,1024]{1,0:T(8,128)(2,1)S(1)}, u32[]{:S(2)}, u32[]{:S(2)}) collective-permute-start(bf16[288,1024]{1,0:T(8,128)(2,1)} %get-tuple-element.59), channel_id=1, source_target_pairs={{0,8},{1,9},{2,10},{3,11},{4,12},{5,13},{6,14},{7,15},{8,0},{9,1},... | collective-permute-start | bytes 1769480 | tf_op jit(solution)/shard_map/ppermute | solution.py:28
  156.0 26.6 %collective-permute-start.20 = (bf16[288,1024]{1,0:T(8,128)(2,1)}, bf16[288,1024]{1,0:T(8,128)(2,1)S(1)}, u32[]{:S(2)}, u32[]{:S(2)}) collective-permute-start(bf16[288,1024]{1,0:T(8,128)(2,1)} %get-tuple-element.60), channel_id=1, source_target_pairs={{0,4},{1,5},{2,6},{3,7},{4,8},{5,9},{6,10},{7,11},{8,12},{9,13},{1... | collective-permute-start | bytes 1769480 | tf_op jit(solution)/shard_map/ppermute | solution.py:28
  156.0 51.6 %collective-permute-start.12 = (bf16[296,1024]{1,0:T(8,128)(2,1)}, bf16[296,1024]{1,0:T(8,128)(2,1)S(1)}, u32[]{:S(2)}, u32[]{:S(2)}) collective-permute-start(bf16[296,1024]{1,0:T(8,128)(2,1)} %get-tuple-element.50), channel_id=1, source_target_pairs={{0,3},{1,0},{2,1},{3,2},{4,7},{5,4},{6,5},{7,6},{8,11},{9,8},{10,9... | collective-permute-start | bytes 1818632 | tf_op jit(solution)/shard_map/ppermute | solution.py:28
  170.3 37.3 %collective-permute-start.13 = (bf16[296,1024]{1,0:T(8,128)(2,1)}, bf16[296,1024]{1,0:T(8,128)(2,1)S(1)}, u32[]{:S(2)}, u32[]{:S(2)}) collective-permute-start(bf16[296,1024]{1,0:T(8,128)(2,1)} %get-tuple-element.51), channel_id=1, source_target_pairs={{0,2},{1,3},{2,0},{3,1},{4,6},{5,7},{6,4},{7,5},{8,10},{9,11},{10,... | collective-permute-start | bytes 1818632 | tf_op jit(solution)/shard_map/ppermute | solution.py:28
  173.8 33.8 %collective-permute-start.14 = (bf16[296,1024]{1,0:T(8,128)(2,1)}, bf16[296,1024]{1,0:T(8,128)(2,1)S(1)}, u32[]{:S(2)}, u32[]{:S(2)}) collective-permute-start(bf16[296,1024]{1,0:T(8,128)(2,1)} %get-tuple-element.52), channel_id=1, source_target_pairs={{0,1},{1,2},{2,3},{3,0},{4,5},{5,6},{6,7},{7,4},{8,9},{9,10},{10,1... | collective-permute-start | bytes 1818632 | tf_op jit(solution)/shard_map/ppermute | solution.py:28
  188.1 24.0 %collective-permute-start.21 = (bf16[128,1024]{1,0:T(8,128)(2,1)S(1)}, bf16[128,1024]{1,0:T(8,128)(2,1)S(1)}, u32[]{:S(2)}, u32[]{:S(2)}) collective-permute-start(bf16[128,1024]{1,0:T(8,128)(2,1)S(1)} %get-tuple-element.62), channel_id=1, source_target_pairs={{0,3},{1,0},{2,1},{3,2},{4,7},{5,4},{6,5},{7,6},{8,11},{9,8},{10,9... | collective-permute-start | bytes 786440 | tf_op jit(solution)/shard_map/ppermute | solution.py:28
  204.0 9.3 %collective-permute-start.22 = (bf16[128,1024]{1,0:T(8,128)(2,1)}, bf16[128,1024]{1,0:T(8,128)(2,1)S(1)}, u32[]{:S(2)}, u32[]{:S(2)}) collective-permute-start(bf16[128,1024]{1,0:T(8,128)(2,1)} %get-tuple-element.63), channel_id=1, source_target_pairs={{0,2},{1,3},{2,0},{3,1},{4,6},{5,7},{6,4},{7,5},{8,10},{9,11},{10,... | collective-permute-start | bytes 786440 | tf_op jit(solution)/shard_map/ppermute | solution.py:28
  207.6 12.6 %collective-permute-start.23 = (bf16[128,1024]{1,0:T(8,128)(2,1)}, bf16[128,1024]{1,0:T(8,128)(2,1)}, u32[]{:S(2)}, u32[]{:S(2)}) collective-permute-start(bf16[128,1024]{1,0:T(8,128)(2,1)} %get-tuple-element.64), channel_id=1, source_target_pairs={{0,1},{1,2},{2,3},{3,0},{4,5},{5,6},{6,7},{7,4},{8,9},{9,10},{10,1... | collective-permute-start | bytes 786440 | tf_op jit(solution)/shard_map/ppermute | solution.py:28
  211.4 8.8 %collective-permute-start.15 = (bf16[136,1024]{1,0:T(8,128)(2,1)}, bf16[136,1024]{1,0:T(8,128)(2,1)S(1)}, u32[]{:S(2)}, u32[]{:S(2)}) collective-permute-start(bf16[136,1024]{1,0:T(8,128)(2,1)} %get-tuple-element.54), channel_id=1, source_target_pairs={{0,12},{1,13},{2,14},{3,15},{4,0},{5,1},{6,2},{7,3},{8,4},{9,5},{1... | collective-permute-start | bytes 835592 | tf_op jit(solution)/shard_map/ppermute | solution.py:28
  212.1 15.4 %collective-permute-start.17 = (bf16[136,1024]{1,0:T(8,128)(2,1)}, bf16[136,1024]{1,0:T(8,128)(2,1)S(1)}, u32[]{:S(2)}, u32[]{:S(2)}) collective-permute-start(bf16[136,1024]{1,0:T(8,128)(2,1)} %get-tuple-element.56), channel_id=1, source_target_pairs={{0,4},{1,5},{2,6},{3,7},{4,8},{5,9},{6,10},{7,11},{8,12},{9,13},{1... | collective-permute-start | bytes 835592 | tf_op jit(solution)/shard_map/ppermute | solution.py:28
  230.8 26.6 %collective-permute-start.24 = (bf16[128,2048]{1,0:T(8,128)(2,1)S(1)}, bf16[128,2048]{1,0:T(8,128)(2,1)S(1)}, u32[]{:S(2)}, u32[]{:S(2)}) collective-permute-start(bf16[128,2048]{1,0:T(8,128)(2,1)S(1)} %get-tuple-element.65), channel_id=1, source_target_pairs={{16,0},{32,16},{48,32},{64,48},{80,64},{96,80},{112,96},{17,1},{33... | collective-permute-start | bytes 1572872 | tf_op jit(solution)/shard_map/ppermute | solution.py:415
  (23 other events, 118.1 us)

commit v2 on v1

v2 whole, which is shorter than its diff:
```python
import functools

import jax
import jax.numpy as jnp
from jax import lax
from jax.experimental import pallas as pl
from jax.experimental.pallas import tpu as pltpu
from jax.sharding import PartitionSpec as P

SIDE = 4
CAP = 72
GROUP = SIDE * CAP
META = 8
BF16 = jnp.bfloat16
F32 = jnp.float32
VMEM = pl.BlockSpec(memory_space=pltpu.VMEM)
SMEM = pl.BlockSpec(memory_space=pltpu.SMEM)
BY_COLS = (((1,), (1,)), ((), ()))
BY_ROWS = (((0,), (0,)), ((), ()))


def shift(block, down, over):
    route = []
    for row in range(SIDE):
        for col in range(SIDE):
            to = (row + down) % SIDE * SIDE + (col + over) % SIDE
            route.append((row * SIDE + col, to))
    return lax.ppermute(block, "expert", route)


def params(mib=56):
    return pltpu.CompilerParams(vmem_limit_bytes=mib * 1024 * 1024)


def cost(flops, nbytes):
    return pl.CostEstimate(flops=flops, bytes_accessed=nbytes, transcendentals=0)


def slots(id_blocks, experts):
    hits = []
    for ids, expert in zip(id_blocks, experts):
        hits.append(jnp.sum(jnp.where(ids == expert, 1.0, 0.0), axis=0, keepdims=True))
    hit = jnp.concatenate(hits, axis=0)
    pad = -len(hits) % 8
    if pad:
        hit = jnp.concatenate([hit, jnp.zeros((pad, hit.shape[1]), F32)], axis=0)
    tokens = hit.shape[1]
    earlier = lax.broadcasted_iota(jnp.int32, (tokens, tokens), 0) < lax.broadcasted_iota(
        jnp.int32, (tokens, tokens), 1
    )
    before = jnp.where(earlier, 1.0, 0.0).astype(BF16)
    rank = jnp.dot(hit.astype(BF16), before, preferred_element_type=F32)
    slot = jnp.where(hit > 0.5, rank, -1.0)
    return [slot[i : i + 1] for i in range(len(hits))]


def one_hot(slot, rows, first=0):
    row = lax.broadcasted_iota(jnp.int32, (rows, slot.shape[1]), 0)
    wanted = jnp.where(slot >= 0.0, slot + first, -1.0).astype(jnp.int32)
    return jnp.where(row == wanted, 1.0, 0.0)


def as_float(expert):
    return expert.astype(F32)


def after(value, *others):
    return lax.optimization_barrier((value, *others))[0]


def ahead(me, down, over):
    row = lax.rem(lax.shift_right_logical(me, 2) + down, SIDE)
    col = lax.rem(lax.bitwise_and(me, SIDE - 1) + over, SIDE)
    return row * SIDE + col


def pack_kernel(x_ref, g_ref, ids_ref, gates_ref, a_ref, b_ref, ids, gates, sems):
    tokens, width = a_ref.shape[0] - META, a_ref.shape[1]
    copies = [
        pltpu.make_async_copy(ids_ref, ids, sems.at[0]),
        pltpu.make_async_copy(gates_ref, gates, sems.at[1]),
        pltpu.make_async_copy(x_ref, a_ref.at[0:tokens], sems.at[2]),
        pltpu.make_async_copy(g_ref, b_ref.at[0:tokens], sems.at[3]),
    ]
    for copy in copies:
        copy.start()
    for copy in copies:
        copy.wait()
    meta = jnp.concatenate(
        [
            ids[...].astype(F32),
            gates[...].astype(F32),
            jnp.zeros((META, width - 2 * tokens), F32),
        ],
        axis=1,
    ).astype(BF16)
    a_ref[tokens : tokens + META] = meta
    b_ref[tokens : tokens + META] = meta


def pack(x, g, ids, gates):
    tokens, width = x.shape
    out = jax.ShapeDtypeStruct((tokens + META, width), BF16)
    return pl.pallas_call(
        pack_kernel,
        out_shape=(out, out),
        in_specs=[pl.BlockSpec(memory_space=pl.ANY)] * 4,
        out_specs=(VMEM, VMEM),
        scratch_shapes=[
            pltpu.VMEM(ids.shape, jnp.int32),
            pltpu.VMEM(gates.shape, BF16),
            pltpu.SemaphoreType.DMA((4,)),
        ],
        compiler_params=params(56),
        cost_estimate=cost(0, 4 * tokens * width * 2),
    )(x, g, ids, gates)


def select_kernel(tokens, step, who_ref, *refs):
    a_refs, b_refs, (a_out, b_out) = refs[:4], refs[4:8], refs[8:]
    width = a_out.shape[1]
    ids = [r[tokens : tokens + META, 0:tokens].astype(F32) for r in (*a_refs, *b_refs)]
    me = who_ref[0]
    experts = [as_float(ahead(me, 0, step))] * 4 + [as_float(ahead(me, step, 0))] * 4
    slot = slots(ids, experts)
    for refs_of, out, part in ((a_refs, a_out, slot[:4]), (b_refs, b_out, slot[4:])):
        picks = [one_hot(s, CAP).astype(BF16) for s in part]
        for left in range(0, width, 512):
            rows = [
                jnp.dot(p, r[0:tokens, left : left + 512], preferred_element_type=F32)
                for p, r in zip(picks, refs_of)
            ]
            out[0:GROUP, left : left + 512] = jnp.concatenate(rows, axis=0).astype(BF16)
    meta = [r[tokens : tokens + META, 0 : 2 * tokens].astype(F32) for r in a_refs]
    meta.append(jnp.zeros((META, width - 8 * tokens), F32))
    a_out[GROUP : GROUP + META] = jnp.concatenate(meta, axis=1).astype(BF16)


def select(who, step, a, b, tokens):
    width = a[0].shape[1]
    return pl.pallas_call(
        functools.partial(select_kernel, tokens, step),
        out_shape=(
            jax.ShapeDtypeStruct((GROUP + META, width), BF16),
            jax.ShapeDtypeStruct((GROUP, width), BF16),
        ),
        in_specs=[SMEM] + [VMEM] * 8,
        out_specs=(VMEM, VMEM),
        compiler_params=params(6),
        cost_estimate=cost(4 * GROUP * tokens * width, 7_000_000),
    )(who, *a, *b)


def ready_kernel(tokens, who_ref, a_ref, b_ref, wg, wu, wdt, pg, pu, db, gate, slot_out):
    me = as_float(who_ref[0])
    ids, value = [], []
    for near in range(SIDE):
        left = 2 * tokens * near
        block = a_ref[GROUP : GROUP + META, left : left + 2 * tokens].astype(F32)
        ids.append(block[:, 0:tokens])
        hit = block[:, 0:tokens] == me
        value.append(
            jnp.sum(jnp.where(hit, block[:, tokens : 2 * tokens], 0.0), axis=0, keepdims=True)
        )
    slot = slots(ids, [me] * SIDE)
    columns = [
        jnp.sum(one_hot(s, CAP) * v, axis=1, keepdims=True) for s, v in zip(slot, value)
    ]
    gate[...] = jnp.broadcast_to(jnp.concatenate(columns, axis=0), gate.shape)
    slot_out[...] = jnp.concatenate(slot + [jnp.zeros((8 - SIDE, tokens), F32)], axis=0)
    for left in range(0, pg.shape[1], 256):
        cols = slice(left, left + 256)
        rows = a_ref[0:GROUP]
        pg[:, cols] = jnp.dot(rows, wg[:, cols], preferred_element_type=F32)
        pu[:, cols] = jnp.dot(rows, wu[:, cols], preferred_element_type=F32)
        db[:, cols] = jnp.dot(b_ref[...], wdt[:, cols], preferred_element_type=F32)


def ready(who, a, b, wg, wu, wdt, tokens):
    width, hidden = wg.shape
    wide = jax.ShapeDtypeStruct((GROUP, hidden), F32)
    return pl.pallas_call(
        functools.partial(ready_kernel, tokens),
        out_shape=(
            wide,
            wide,
            wide,
            jax.ShapeDtypeStruct((GROUP, 128), F32),
            jax.ShapeDtypeStruct((8, tokens), F32),
        ),
        in_specs=[SMEM] + [VMEM] * 5,
        out_specs=[VMEM] * 5,
        compiler_params=params(8),
        cost_estimate=cost(6 * GROUP * width * hidden, 6_000_000),
    )(who, a, b, wg, wu, wdt)


def middle_kernel(tokens, *refs):
    pgs, pus, dbs, gates, slot_refs = (refs[4 * i : 4 * i + 4] for i in range(5))
    wgt, wut = refs[20:22]
    gg_out, gu_out, hg_out = refs[22:25]
    first_out, second_out = refs[25:29], refs[29:33]
    gg, gu, hg, back, slot_sum = refs[33:]
    half = first_out[0].shape[1]
    hidden_units = gg.shape[1]
    for k in range(SIDE):
        lines = []
        for near in range(SIDE):
            here = slice(near * CAP, (near + 1) * CAP)
            there = slice(k * CAP, (k + 1) * CAP)
            total = jnp.zeros((CAP, 1), F32)
            weight = gates[k][here, 0:1]
            for left in range(0, hidden_units, 256):
                cols = slice(left, left + 256)
                pre_gate, pre_up = pgs[k][here, cols], pus[k][here, cols]
                down_back = dbs[near][there, cols]
                sig = jax.nn.sigmoid(pre_gate)
                active = pre_gate * sig
                hidden = active * pre_up
                total += jnp.sum(hidden * down_back, axis=1, keepdims=True)
                scaled = weight * down_back
                gg[here, cols] = scaled * pre_up * sig * (1.0 + pre_gate * (1.0 - sig))
                gu[here, cols] = scaled * active
                row = near * GROUP + k * CAP
                hg[row : row + CAP, cols] = weight * hidden
            slot = slot_refs[k][near : near + 1]
            value = total.astype(BF16).astype(F32)
            lines.append(jnp.sum(one_hot(slot, CAP) * value, axis=0, keepdims=True))
        at = slice(k * GROUP, (k + 1) * GROUP)
        grad_gate, grad_up = gg[...].astype(BF16), gu[...].astype(BF16)
        gg_out[at] = grad_gate
        gu_out[at] = grad_up
        for left in range(0, 2 * half, 512):
            cols = slice(left, left + 512)
            rows = jnp.dot(grad_gate, wgt[:, cols], preferred_element_type=F32) + jnp.dot(
                grad_up, wut[:, cols], preferred_element_type=F32
            )
            if left < half:
                first_out[k][0:GROUP, cols] = rows.astype(BF16)
            else:
                back[at, left - half : left - half + 512] = rows
        lines.append(jnp.zeros((META - SIDE, tokens), F32))
        table = jnp.concatenate(lines, axis=0)
        table = jnp.concatenate([table, jnp.zeros((META, half - tokens), F32)], axis=1)
        first_out[k][GROUP : GROUP + META] = table.astype(BF16)
    for near in range(SIDE):
        rows = [back[k * GROUP + near * CAP : k * GROUP + (near + 1) * CAP] for k in range(SIDE)]
        second_out[near][...] = jnp.concatenate(rows, axis=0).astype(BF16)
    hg_out[...] = hg[...].astype(BF16)


def middle(pg, pu, db, gate, slot, wgt, wut, tokens):
    hidden, width = wgt.shape
    rows, half = SIDE * GROUP, width // 2
    return pl.pallas_call(
        functools.partial(middle_kernel, tokens),
        out_shape=(
            [jax.ShapeDtypeStruct((rows, hidden), BF16)] * 3
            + [jax.ShapeDtypeStruct((GROUP + META, half), BF16)] * SIDE
            + [jax.ShapeDtypeStruct((GROUP, half), BF16)] * SIDE
        ),
        in_specs=[VMEM] * 22,
        out_specs=[VMEM] * 11,
        scratch_shapes=[
            pltpu.VMEM((GROUP, hidden), F32),
            pltpu.VMEM((GROUP, hidden), F32),
            pltpu.VMEM((rows, hidden), F32),
            pltpu.VMEM((rows, half), F32),
            pltpu.VMEM((rows, 1), F32),
        ],
        compiler_params=params(14),
        cost_estimate=cost(4 * rows * width * hidden, 10_000_000),
    )(*pg, *pu, *db, *gate, *slot, wgt, wut)


def up_wgrad_kernel(*refs):
    a_refs, (gg, gu), (gate_out, up_out) = refs[:4], refs[4:6], refs[6:]
    a = jnp.concatenate([r[0:GROUP] for r in a_refs], axis=0)
    gate_out[...] = lax.dot_general(a, gg[...], BY_ROWS, preferred_element_type=F32).astype(BF16)
    up_out[...] = lax.dot_general(a, gu[...], BY_ROWS, preferred_element_type=F32).astype(BF16)


def up_wgrads(a, gg, gu):
    rows, hidden = gg.shape
    width = a[0].shape[1]
    tile = 256
    whole = pl.BlockSpec((rows, hidden), lambda d: (0, 0), pipeline_mode=pl.Buffered(1))
    return pl.pallas_call(
        up_wgrad_kernel,
        grid=(width // tile,),
        out_shape=[jax.ShapeDtypeStruct((width, hidden), BF16)] * 2,
        in_specs=[pl.BlockSpec((GROUP + META, tile), lambda d: (0, d))] * SIDE + [whole] * 2,
        out_specs=[pl.BlockSpec((tile, hidden), lambda d: (d, 0))] * 2,
        compiler_params=params(20),
        cost_estimate=cost(4 * rows * width * hidden, 15_000_000),
    )(*a, gg, gu)


def down_wgrad_kernel(*refs):
    b_refs, (hg, down_out) = refs[:4], refs[4:]
    b = jnp.concatenate([r[...] for r in b_refs], axis=0)
    down_out[...] = lax.dot_general(hg[...], b, BY_ROWS, preferred_element_type=F32).astype(BF16)


def down_wgrads(b, hg):
    rows, hidden = hg.shape
    width = b[0].shape[1]
    tile = 512
    return pl.pallas_call(
        down_wgrad_kernel,
        grid=(width // tile,),
        out_shape=jax.ShapeDtypeStruct((hidden, width), BF16),
        in_specs=[pl.BlockSpec((GROUP, tile), lambda d: (0, d))] * SIDE
        + [pl.BlockSpec((rows, hidden), lambda d: (0, 0), pipeline_mode=pl.Buffered(1))],
        out_specs=pl.BlockSpec((hidden, tile), lambda d: (0, d)),
        compiler_params=params(20),
        cost_estimate=cost(2 * rows * width * hidden, 10_000_000),
    )(*b, hg)


def gather_kernel(tokens, along_row, who_ref, *refs):
    id_refs, back_refs, outs = refs[:4], refs[4:8], refs[8:]
    half = back_refs[0].shape[1]
    ids = [r[tokens : tokens + META, 0:tokens].astype(F32) for r in id_refs]
    pairs = [(near, far) for near in range(SIDE) for far in range(SIDE)]
    me = who_ref[0]
    experts = [as_float(ahead(me, 0, f) if along_row else ahead(me, f, 0)) for f in range(SIDE)]
    slot = slots([ids[n] for n, _ in pairs], [experts[f] for _, f in pairs])
    for near in range(SIDE):
        places = []
        for far in range(SIDE):
            spread = one_hot(slot[near * SIDE + far], GROUP, near * CAP)
            places.append(spread.T.astype(BF16))
        for left in range(0, half, 512):
            cols = slice(left, left + 512)
            part = jnp.dot(places[0], back_refs[0][0:GROUP, cols], preferred_element_type=F32)
            for far in range(1, SIDE):
                part += jnp.dot(
                    places[far], back_refs[far][0:GROUP, cols], preferred_element_type=F32
                )
            outs[near][0:tokens, cols] = part.astype(BF16)
        if along_row:
            lines = [
                r[GROUP : GROUP + META, 0:tokens].astype(F32)[near : near + 1] for r in back_refs
            ]
            lines.append(jnp.zeros((META - SIDE, tokens), F32))
            table = jnp.concatenate(lines, axis=0)
            table = jnp.concatenate([table, jnp.zeros((META, half - tokens), F32)], axis=1)
            outs[near][tokens : tokens + META] = table.astype(BF16)


def gather(who, blocks, back, tokens, along_row):
    half = back[0].shape[1]
    rows = tokens + META if along_row else tokens
    return pl.pallas_call(
        functools.partial(gather_kernel, tokens, along_row),
        out_shape=[jax.ShapeDtypeStruct((rows, half), BF16)] * SIDE,
        in_specs=[SMEM] + [VMEM] * 8,
        out_specs=[VMEM] * SIDE,
        compiler_params=params(8),
        cost_estimate=cost(32 * tokens * GROUP * half, 6_000_000),
    )(who, *blocks, *back)


def finish_kernel(tokens, who_ref, g_ref, ids_ref, *refs):
    firsts, seconds, (out, gate_out) = refs[:4], refs[4:8], refs[8:]
    half = firsts[0].shape[1]
    for parts, left in ((firsts, 0), (seconds, half)):
        cols = slice(left, left + half)
        moe = parts[0][0:tokens].astype(F32)
        for part in parts[1:]:
            moe += part[0:tokens].astype(F32)
        moe = moe.astype(BF16).astype(F32)
        out[:, cols] = (g_ref[:, cols].astype(F32) + moe).astype(BF16)
    ids, me = ids_ref[...], who_ref[0]
    grad = jnp.zeros(ids.shape, F32)
    for near in range(SIDE):
        table = firsts[near][tokens : tokens + META, 0:tokens].astype(F32)
        for far in range(SIDE):
            grad += jnp.where(ids == ahead(me, near, far), table[far : far + 1], 0.0)
    gate_out[...] = grad.astype(BF16)


def finish(who, g, ids, firsts, seconds):
    tokens, width = g.shape
    return pl.pallas_call(
        functools.partial(finish_kernel, tokens),
        out_shape=(
            jax.ShapeDtypeStruct((tokens, width), BF16),
            jax.ShapeDtypeStruct(ids.shape, BF16),
        ),
        in_specs=[SMEM] + [VMEM] * 10,
        out_specs=(VMEM, VMEM),
        compiler_params=params(16),
        cost_estimate=cost(0, 3_500_000),
    )(who, g, ids, *firsts, *seconds)


def exchange(one, two, one_route, two_route, meanwhile=lambda: ()):
    one, two = list(one), list(two)
    for d in (1, 3, 2):
        one[d] = shift(one[d], *one_route(d))
    for d in (1, 3):
        two[d] = shift(two[d], *two_route(d))
    two[2] = shift(after(two[2], two[1], *meanwhile()), *two_route(2))
    return one, two


def local(inputs, out_grad, expert_ids, gate_probs, gate_weight, up_weight, down_weight):
    x, g = inputs[0], out_grad[0]
    tokens = x.shape[0]
    ids, gates = expert_ids[0].T, gate_probs[0].T
    who = lax.axis_index("expert").astype(jnp.int32)[None]

    a0, b0 = pack(x, g, ids, gates)
    wg, wu, wd = gate_weight[0, 0], up_weight[0, 0], down_weight[0, 0]
    wdt, wut = after(wd, a0).T, after(wu, a0).T
    a, b = exchange([a0] * SIDE, [b0] * SIDE, lambda d: (d, 0), lambda d: (0, d), lambda: (wdt,))
    wgt = after(wg, wut).T

    send_a, send_b, turn = [None] * SIDE, [None] * SIDE, after(who, wgt)
    for d in (1, 3, 2, 0):
        send_a[d], send_b[d] = select(turn, d, a, b, tokens)
        turn = after(who, send_a[d])
    own = ready(who, send_a[0], send_b[0], wg, wu, wdt, tokens)
    rows_in, rows_grad = exchange(
        send_a, send_b, lambda d: (0, d), lambda d: (d, 0), lambda: own[-1:]
    )

    made = [own]
    for d in (1, 2, 3):
        made.append(ready(who, rows_in[d], rows_grad[d], wg, wu, wdt, tokens))
    made = middle(*zip(*made), wgt, wut, tokens)
    gg, gu, hg = made[:3]
    down_wgrad = down_wgrads(rows_grad, hg)
    first, second = exchange(
        made[3:7], made[7:11], lambda d: (0, -d), lambda d: (-d, 0), lambda: (down_wgrad,)
    )
    gate_wgrad, up_wgrad = up_wgrads(rows_in, gg, gu)

    turn = after(who, gate_wgrad)
    first = gather(turn, a, first, tokens, True)
    second = gather(turn, b, second, tokens, False)
    first, second = exchange(first, second, lambda d: (-d, 0), lambda d: (0, -d))
    section_grad, gate_grad = finish(who, g, ids, first, second)

    sections = lax.axis_size("section")
    handed = lax.ppermute(section_grad, "section", [(i + 1, i) for i in range(sections - 1)])
    return (
        handed[None],
        gate_grad.T[None],
        gate_wgrad[None, None],
        up_wgrad[None, None],
        down_wgrad[None, None],
    )


def solution(mesh):
    rows, mats = P("section", "expert", None), P("section", "expert", None, None)
    return jax.shard_map(
        local,
        mesh=mesh,
        in_specs=(rows, rows, rows, rows, mats, mats, mats),
        out_specs=(rows, rows, mats, mats, mats),
        check_vma=False,
    )
```

time: 260 us -> 202 us (0.78)
  starting transfers between devices: 80.7 us -> 47.1 us
  Pallas kernels: 80.9 us -> 70 us
  waiting for transfers between devices: 72.2 us -> 64.9 us
  other arithmetic: 5.34 us -> 0 us
  local copies, waits for them, and re-layouts: 18.2 us -> 15.2 us
    ppermute x24, starting transfers between devices: 78.1 us -> 33.5 us  [shift(): return lax.ppermute(block, 'expert', route)]
    ppermute x24, waiting for transfers between devices: 72.2 us -> 57 us  [shift(): return lax.ppermute(block, 'expert', route)]
    ppermute x1, starting transfers between devices: 2.63 us -> 13.6 us  [local(): lax.ppermute(section_grad, 'section', [(i + 1, i) for i in range(sections...]
    pallas_call x9 -> x14, Pallas kernels: 79.2 us -> 69.3 us  [the longest x1 18.1 us: middle(): pl.pallas_call(functools.partial(middle_kernel, tokens), out_shape=[jax.S...]
    ppermute x1, waiting for transfers between devices: 0.01 us -> 7.94 us  [local(): lax.ppermute(section_grad, 'section', [(i + 1, i) for i in range(sections...]
    another operation x2 -> x0, other arithmetic: 5.22 us -> none  [local(): send_a, send_b = select(jnp.stack([same_row[d], same_col[d]]), a, b, tokens)]
    unnamed x45 -> x26, local copies, waits for them, and re-layouts: 16.9 us -> 15.2 us
  transfers between devices with their start and end apart: 25 -> 25, of which waited for: 11 -> 13; matrix products, arithmetic and copies ran while one was open for 3% -> 6% of each run, Pallas kernels for 12% -> 22%
where the time goes in v2:
time: 202 us; the launch traced here: 198 us
  Pallas kernels  70 us (35%)
  waiting for transfers between devices  64.9 us (32%)
  starting transfers between devices  47.1 us (23%)
  local copies, waits for them, and re-layouts  15.2 us (8%)
    ppermute x24, waiting for transfers between devices, shift(): return lax.ppermute(block, 'expert', route)  57 us
    ppermute x24, starting transfers between devices, shift(): return lax.ppermute(block, 'expert', route)  33.5 us
    pallas_call x1, Pallas kernels, middle(): pl.pallas_call(functools.partial(middle_kernel, tokens), out_shape=[jax.S...  18.1 us
    unnamed x26, local copies, waits for them, and re-layouts  15.2 us
    ppermute x1, starting transfers between devices, local(): lax.ppermute(section_grad, 'section', [(i + 1, i) for i in range(sections...  13.6 us
    pallas_call x4, Pallas kernels, ready(): pl.pallas_call(functools.partial(ready_kernel, tokens), out_shape=(wide,...  11.9 us
    pallas_call x4, Pallas kernels, select(): pl.pallas_call(functools.partial(select_kernel, tokens, step), out_shape=...  11.7 us
    pallas_call x1, Pallas kernels, up_wgrads(): pl.pallas_call(up_wgrad_kernel, grid=(width // tile,), out_shape=[jax.Sha...  11.2 us
  transfers between devices with their start and end apart: 25, of which 13 were waited for; matrix products, arithmetic and copies ran while one was open for 6% of the time, Pallas kernels for 22%

profile of v2, /device:TPU:1, one launch (start us, length us, event | category | flops | bytes accessed | tf_op | source)
XLA Modules:
  0.0 198.2 jit_solution(15859895687517649567)
XLA Ops:
  11.4 4.8 %copy.14 = bf16[1,1,768,2048]{2,3,1,0:T(8,128)(2,1)} copy(bf16[1,1,768,2048]{3,2,1,0:T(8,128)(2,1)} %param.13) | data formatting | bytes 6291456 | tf_op args[6]
  16.2 4.0 %collective-permute-done.3.refs_5_.refs_1_ = bf16[136,2048]{1,0:T(8,128)(2,1)} collective-permute-done((bf16[136,2048]{1,0:T(8,128)(2,1)}, bf16[136,2048]{1,0:T(8,128)(2,1)}, u32[]{:S(2)}, u32[]{:S(2)}) %collective-permute-start.3) | collective-permute-done | bytes 557088 | tf_op jit(solution)/shard_map/ppermute | solution.py:28
  24.1 4.6 %copy.13 = bf16[1,1,2048,768]{2,3,1,0:T(8,128)(2,1)} copy(bf16[1,1,2048,768]{3,2,1,0:T(8,128)(2,1)} %param.12) | data formatting | bytes 6291456 | tf_op args[5]
  28.7 10.0 %collective-permute-done.refs_1_ = bf16[136,2048]{1,0:T(8,128)(2,1)} collective-permute-done((bf16[136,2048]{1,0:T(8,128)(2,1)}, bf16[136,2048]{1,0:T(8,128)(2,1)}, u32[]{:S(2)}, u32[]{:S(2)}) %collective-permute-start) | collective-permute-done | bytes 557088 | tf_op jit(solution)/shard_map/ppermute | solution.py:28
  40.8 2.9 %shard_map.111 = (bf16[296,2048]{1,0:T(8,128)(2,1)S(1)}, bf16[288,2048]{1,0:T(8,128)(2,1)S(1)}) custom-call(s32[1]{0:T(128)} %bitcast.who_ref, bf16[136,2048]{1,0:T(8,128)(2,1)S(1)} %copy-done.3, bf16[136,2048]{1,0:T(8,128)(2,1)} %collective-permute-done.refs_1_, bf16[136,2048]{1,0:T(8,128)(2,1)} %collective-permute-done.1.refs_2_, ...), custom_call_target="tpu_custom_call" | custom-call | flops 301989888 | bytes 7000000 | tf_op jit(solution)/shard_map/pallas_call | solution.py:141
  43.9 2.9 %shard_map.112 = (bf16[296,2048]{1,0:T(8,128)(2,1)S(1)}, bf16[288,2048]{1,0:T(8,128)(2,1)S(1)}) custom-call(s32[1]{0:T(128)} %bitcast.who_ref, bf16[136,2048]{1,0:T(8,128)(2,1)S(1)} %copy-done.3, bf16[136,2048]{1,0:T(8,128)(2,1)} %collective-permute-done.refs_1_, bf16[136,2048]{1,0:T(8,128)(2,1)} %collective-permute-done.1.refs_2_, ...), custom_call_target="tpu_custom_call" | custom-call | flops 301989888 | bytes 7000000 | tf_op jit(solution)/shard_map/pallas_call | solution.py:141
  49.5 3.0 %shard_map.113 = (bf16[296,2048]{1,0:T(8,128)(2,1)S(1)}, bf16[288,2048]{1,0:T(8,128)(2,1)S(1)}) custom-call(s32[1]{0:T(128)} %bitcast.who_ref, bf16[136,2048]{1,0:T(8,128)(2,1)S(1)} %copy-done.3, bf16[136,2048]{1,0:T(8,128)(2,1)} %collective-permute-done.refs_1_, bf16[136,2048]{1,0:T(8,128)(2,1)} %collective-permute-done.1.refs_2_, ...), custom_call_target="tpu_custom_call" | custom-call | flops 301989888 | bytes 7000000 | tf_op jit(solution)/shard_map/pallas_call | solution.py:141
  55.2 2.9 %shard_map.114 = (bf16[296,2048]{1,0:T(8,128)(2,1)S(1)}, bf16[288,2048]{1,0:T(8,128)(2,1)S(1)}) custom-call(s32[1]{0:T(128)} %bitcast.who_ref, bf16[136,2048]{1,0:T(8,128)(2,1)S(1)} %copy-done.3, bf16[136,2048]{1,0:T(8,128)(2,1)} %collective-permute-done.refs_1_, bf16[136,2048]{1,0:T(8,128)(2,1)} %collective-permute-done.1.refs_2_, ...), custom_call_target="tpu_custom_call" | custom-call | flops 301989888 | bytes 7000000 | tf_op jit(solution)/shard_map/pallas_call | solution.py:141
  58.1 3.0 %shard_map.115 = (f32[288,768]{1,0:T(8,128)S(1)}, f32[288,768]{1,0:T(8,128)S(1)}, f32[288,768]{1,0:T(8,128)S(1)}, f32[288,128]{1,0:T(8,128)S(1)}, f32[8,128]{1,0:T(8,128)S(1)}) custom-call(s32[1]{0:T(128)} %bitcast.who_ref, bf16[296,2048]{1,0:T(8,128)(2,1)S(1)} %get-tuple-element.83.a_ref.refs_0_, bf16[288,2048]{1,0:T(8,128)(2,1)S(1)} %get-tuple-element.84.b_ref.refs_0_, ...), custom_call_target="tpu_custom_call" | custom-call | flops 2717908992 | bytes 6000000 | tf_op jit(solution)/shard_map/pallas_call | solution.py:182
  61.1 10.9 %collective-permute-done.9.b_ref.refs_1_ = bf16[288,2048]{1,0:T(8,128)(2,1)S(1)} collective-permute-done((bf16[288,2048]{1,0:T(8,128)(2,1)S(1)}, bf16[288,2048]{1,0:T(8,128)(2,1)S(1)}, u32[]{:S(2)}, u32[]{:S(2)}) %collective-permute-start.9) | collective-permute-done | bytes 1179680 | tf_op jit(solution)/shard_map/ppermute | solution.py:28
  72.9 3.0 %shard_map.116 = (f32[288,768]{1,0:T(8,128)S(1)}, f32[288,768]{1,0:T(8,128)S(1)}, f32[288,768]{1,0:T(8,128)S(1)}, f32[288,128]{1,0:T(8,128)S(1)}, f32[8,128]{1,0:T(8,128)S(1)}) custom-call(s32[1]{0:T(128)} %bitcast.who_ref, bf16[296,2048]{1,0:T(8,128)(2,1)S(1)} %collective-permute-done.6.a_ref.refs_1_, ...), custom_call_target="tpu_custom_call" | custom-call | flops 2717908992 | bytes 6000000 | tf_op jit(solution)/shard_map/pallas_call | solution.py:182
  75.9 3.7 %collective-permute-done.11.b_ref.refs_3_ = bf16[288,2048]{1,0:T(8,128)(2,1)S(1)} collective-permute-done((bf16[288,2048]{1,0:T(8,128)(2,1)S(1)}, bf16[288,2048]{1,0:T(8,128)(2,1)S(1)}, u32[]{:S(2)}, u32[]{:S(2)}) %collective-permute-start.11) | collective-permute-done | bytes 1179680 | tf_op jit(solution)/shard_map/ppermute | solution.py:28
  79.6 3.0 %shard_map.118 = (f32[288,768]{1,0:T(8,128)S(1)}, f32[288,768]{1,0:T(8,128)S(1)}, f32[288,768]{1,0:T(8,128)S(1)}, f32[288,128]{1,0:T(8,128)S(1)}, f32[8,128]{1,0:T(8,128)S(1)}) custom-call(s32[1]{0:T(128)} %bitcast.who_ref, bf16[296,2048]{1,0:T(8,128)(2,1)S(1)} %collective-permute-done.8.a_ref.refs_3_, ...), custom_call_target="tpu_custom_call" | custom-call | flops 2717908992 | bytes 6000000 | tf_op jit(solution)/shard_map/pallas_call | solution.py:182
  82.6 16.1 %collective-permute-done.7.a_ref.refs_2_ = bf16[296,2048]{1,0:T(8,128)(2,1)S(1)} collective-permute-done((bf16[296,2048]{1,0:T(8,128)(2,1)S(1)}, bf16[296,2048]{1,0:T(8,128)(2,1)S(1)}, u32[]{:S(2)}, u32[]{:S(2)}) %collective-permute-start.7) | collective-permute-done | bytes 1212448 | tf_op jit(solution)/shard_map/ppermute | solution.py:28
  99.9 3.0 %shard_map.117 = (f32[288,768]{1,0:T(8,128)S(1)}, f32[288,768]{1,0:T(8,128)S(1)}, f32[288,768]{1,0:T(8,128)S(1)}, f32[288,128]{1,0:T(8,128)S(1)}, f32[8,128]{1,0:T(8,128)S(1)}) custom-call(s32[1]{0:T(128)} %bitcast.who_ref, bf16[296,2048]{1,0:T(8,128)(2,1)S(1)} %collective-permute-done.7.a_ref.refs_2_, ...), custom_call_target="tpu_custom_call" | custom-call | flops 2717908992 | bytes 6000000 | tf_op jit(solution)/shard_map/pallas_call | solution.py:182
  102.9 18.1 %shard_map.119 = (bf16[1152,768]{1,0:T(8,128)(2,1)S(1)}, bf16[1152,768]{1,0:T(8,128)(2,1)S(1)}, bf16[1152,768]{1,0:T(8,128)(2,1)S(1)}, bf16[296,1024]{1,0:T(8,12...) custom-call(f32[288,768]{1,0:T(8,128)S(1)} %get-tuple-element.85.ref, ...), custom_call_target="tpu_custom_call" | custom-call | flops 7247757312 | bytes 10000000 | tf_op jit(solution)/shard_map/pallas_call | solution.py:255
  121.0 6.8 %collective-permute-start.18 = (bf16[288,1024]{1,0:T(8,128)(2,1)S(1)}, bf16[288,1024]{1,0:T(8,128)(2,1)S(1)}, u32[]{:S(2)}, u32[]{:S(2)}) collective-permute-start(bf16[288,1024]{1,0:T(8,128)(2,1)S(1)} %get-tuple-element.122), channel_id=1, source_target_pairs={{0,12},{1,13},{2,14},{3,15},{4,0},{5,1},{6,2},{7,3},{8,4},{9,5},{1... | collective-permute-start | bytes 1769480 | tf_op jit(solution)/shard_map/ppermute | solution.py:28
  131.4 6.1 %shard_map.122 = bf16[768,2048]{1,0:T(8,128)(2,1)} custom-call(bf16[288,2048]{1,0:T(8,128)(2,1)S(1)} %get-tuple-element.84.b_ref.refs_0_, bf16[288,2048]{1,0:T(8,128)(2,1)S(1)} %collective-permute-done.9.b_ref.refs_1_, bf16[288,2048]{1,0:T(8,128)(2,1)S(1)} %collective-permute-done.10.b_ref.refs_2_, ...), custom_call_target="tpu_custom_call" | custom-call | flops 3623878656 | bytes 10000000 | tf_op jit(solution)/shard_map/pallas_call | solution.py:309
  139.3 11.2 %shard_map.120 = (bf16[2048,768]{1,0:T(8,128)(2,1)}, bf16[2048,768]{1,0:T(8,128)(2,1)}) custom-call(bf16[296,2048]{1,0:T(8,128)(2,1)S(1)} %get-tuple-element.83.a_ref.refs_0_, bf16[296,2048]{1,0:T(8,128)(2,1)S(1)} %collective-permute-done.6.a_ref.refs_1_, bf16[296,2048]{1,0:T(8,128)(2,1)S(1)} %collective-permute-done.7.a_ref.refs_2_, ...), custom_call_target="tpu_custom_call" | custom-call | flops 7247757312 | bytes 15000000 | tf_op jit(solution)/shard_map/pallas_call | solution.py:288
  150.5 4.0 %shard_map.123 = (bf16[128,1024]{1,0:T(8,128)(2,1)S(1)}, bf16[128,1024]{1,0:T(8,128)(2,1)S(1)}, bf16[128,1024]{1,0:T(8,128)(2,1)S(1)}, bf16[128,1024]{1,0:T(8,128)(2,1)S(1)}) custom-call(s32[1]{0:T(128)} %bitcast.who_ref, bf16[136,2048]{1,0:T(8,128)(2,1)S(1)} %copy-done.6, bf16[136,2048]{1,0:T(8,128)(2,1)} %collective-permute-done.3.refs_5_.refs_1_, ...), custom_call_target="tpu_custom_call" | custom-call | flops 1207959552 | bytes 6000000 | tf_op jit(solution)/shard_map/pallas_call | solution.py:355
  158.9 4.0 %shard_map.121 = (bf16[136,1024]{1,0:T(8,128)(2,1)S(1)}, bf16[136,1024]{1,0:T(8,128)(2,1)S(1)}, bf16[136,1024]{1,0:T(8,128)(2,1)S(1)}, bf16[136,1024]{1,0:T(8,128)(2,1)S(1)}) custom-call(s32[1]{0:T(128)} %bitcast.who_ref, bf16[136,2048]{1,0:T(8,128)(2,1)S(1)} %copy-done.4, bf16[136,2048]{1,0:T(8,128)(2,1)} %collective-permute-done.refs_1_, ...), custom_call_target="tpu_custom_call" | custom-call | flops 1207959552 | bytes 6000000 | tf_op jit(solution)/shard_map/pallas_call | solution.py:355
  171.1 2.9 %collective-permute-done.17.refs_3_ = bf16[136,1024]{1,0:T(8,128)(2,1)S(1)} collective-permute-done((bf16[136,1024]{1,0:T(8,128)(2,1)S(1)}, bf16[136,1024]{1,0:T(8,128)(2,1)S(1)}, u32[]{:S(2)}, u32[]{:S(2)}) %collective-permute-start.17) | collective-permute-done | bytes 278560 | tf_op jit(solution)/shard_map/ppermute | solution.py:28
  175.7 13.6 %collective-permute-start.24 = (bf16[128,2048]{1,0:T(8,128)(2,1)S(1)}, bf16[128,2048]{1,0:T(8,128)(2,1)S(1)}, u32[]{:S(2)}, u32[]{:S(2)}) collective-permute-start(bf16[128,2048]{1,0:T(8,128)(2,1)S(1)} %get-tuple-element.132), channel_id=1, source_target_pairs={{16,0},{32,16},{48,32},{64,48},{80,64},{96,80},{112,96},{17,1},{33... | collective-permute-start | bytes 1572872 | tf_op jit(solution)/shard_map/ppermute | solution.py:448
  189.3 7.9 %collective-permute-done.24 = bf16[128,2048]{1,0:T(8,128)(2,1)S(1)} collective-permute-done((bf16[128,2048]{1,0:T(8,128)(2,1)S(1)}, bf16[128,2048]{1,0:T(8,128)(2,1)S(1)}, u32[]{:S(2)}, u32[]{:S(2)}) %collective-permute-start.24) | collective-permute-done | bytes 524320 | tf_op jit(solution)/shard_map/ppermute | solution.py:448
  (67 shorter events, 44.9 us)
Async XLA Ops:
  2.9 17.3 %collective-permute-start.3 = (bf16[136,2048]{1,0:T(8,128)(2,1)}, bf16[136,2048]{1,0:T(8,128)(2,1)}, u32[]{:S(2)}, u32[]{:S(2)}) collective-permute-start(bf16[136,2048]{1,0:T(8,128)(2,1)} %get-tuple-element.76.refs_4_.refs_0_), channel_id=1, source_target_pairs={{0,1},{1,2},{2,3},{3,0},{4,5},{5,6},{6,7},{7,4},{8,9},{9,10},{10,1... | collective-permute-start | bytes 1671176 | tf_op jit(solution)/shard_map/ppermute | solution.py:28
  5.5 23.3 %collective-permute-start.5 = (bf16[136,2048]{1,0:T(8,128)(2,1)}, bf16[136,2048]{1,0:T(8,128)(2,1)}, u32[]{:S(2)}, u32[]{:S(2)}) collective-permute-start(bf16[136,2048]{1,0:T(8,128)(2,1)} %get-tuple-element.76.refs_4_.refs_0_), channel_id=1, source_target_pairs={{0,3},{1,0},{2,1},{3,2},{4,7},{5,4},{6,5},{7,6},{8,11},{9,8},{10,9... | collective-permute-start | bytes 1671176 | tf_op jit(solution)/shard_map/ppermute | solution.py:28
  7.7 21.1 %collective-permute-start.2 = (bf16[136,2048]{1,0:T(8,128)(2,1)}, bf16[136,2048]{1,0:T(8,128)(2,1)}, u32[]{:S(2)}, u32[]{:S(2)}) collective-permute-start(bf16[136,2048]{1,0:T(8,128)(2,1)} %get-tuple-element.70.refs_0_), channel_id=1, source_target_pairs={{0,12},{1,13},{2,14},{3,15},{4,0},{5,1},{6,2},{7,3},{8,4},{9,5},{1... | collective-permute-start | bytes 1671176 | tf_op jit(solution)/shard_map/ppermute | solution.py:28
  10.4 18.3 %collective-permute-start.1 = (bf16[136,2048]{1,0:T(8,128)(2,1)}, bf16[136,2048]{1,0:T(8,128)(2,1)}, u32[]{:S(2)}, u32[]{:S(2)}) collective-permute-start(bf16[136,2048]{1,0:T(8,128)(2,1)} %get-tuple-element.70.refs_0_), channel_id=1, source_target_pairs={{0,8},{1,9},{2,10},{3,11},{4,12},{5,13},{6,14},{7,15},{8,0},{9,1},... | collective-permute-start | bytes 1671176 | tf_op jit(solution)/shard_map/ppermute | solution.py:28
  10.7 28.0 %collective-permute-start = (bf16[136,2048]{1,0:T(8,128)(2,1)}, bf16[136,2048]{1,0:T(8,128)(2,1)}, u32[]{:S(2)}, u32[]{:S(2)}) collective-permute-start(bf16[136,2048]{1,0:T(8,128)(2,1)} %get-tuple-element.70.refs_0_), channel_id=1, source_target_pairs={{0,4},{1,5},{2,6},{3,7},{4,8},{5,9},{6,10},{7,11},{8,12},{9,13},{1... | collective-permute-start | bytes 1671176 | tf_op jit(solution)/shard_map/ppermute | solution.py:28
  20.3 18.5 %collective-permute-start.4 = (bf16[136,2048]{1,0:T(8,128)(2,1)}, bf16[136,2048]{1,0:T(8,128)(2,1)}, u32[]{:S(2)}, u32[]{:S(2)}) collective-permute-start(bf16[136,2048]{1,0:T(8,128)(2,1)} %get-tuple-element.76.refs_4_.refs_0_), channel_id=1, source_target_pairs={{0,2},{1,3},{2,0},{3,1},{4,6},{5,7},{6,4},{7,5},{8,10},{9,11},{10,... | collective-permute-start | bytes 1671176 | tf_op jit(solution)/shard_map/ppermute | solution.py:28
  43.7 28.3 %collective-permute-start.9 = (bf16[288,2048]{1,0:T(8,128)(2,1)S(1)}, bf16[288,2048]{1,0:T(8,128)(2,1)S(1)}, u32[]{:S(2)}, u32[]{:S(2)}) collective-permute-start(bf16[288,2048]{1,0:T(8,128)(2,1)S(1)} %get-tuple-element.86), channel_id=1, source_target_pairs={{0,4},{1,5},{2,6},{3,7},{4,8},{5,9},{6,10},{7,11},{8,12},{9,13},{1... | collective-permute-start | bytes 3538952 | tf_op jit(solution)/shard_map/ppermute | solution.py:28
  43.8 29.1 %collective-permute-start.6 = (bf16[296,2048]{1,0:T(8,128)(2,1)S(1)}, bf16[296,2048]{1,0:T(8,128)(2,1)S(1)}, u32[]{:S(2)}, u32[]{:S(2)}) collective-permute-start(bf16[296,2048]{1,0:T(8,128)(2,1)S(1)} %get-tuple-element.77), channel_id=1, source_target_pairs={{0,1},{1,2},{2,3},{3,0},{4,5},{5,6},{6,7},{7,4},{8,9},{9,10},{10,1... | collective-permute-start | bytes 3637256 | tf_op jit(solution)/shard_map/ppermute | solution.py:28
  46.8 32.8 %collective-permute-start.8 = (bf16[296,2048]{1,0:T(8,128)(2,1)S(1)}, bf16[296,2048]{1,0:T(8,128)(2,1)S(1)}, u32[]{:S(2)}, u32[]{:S(2)}) collective-permute-start(bf16[296,2048]{1,0:T(8,128)(2,1)S(1)} %get-tuple-element.79), channel_id=1, source_target_pairs={{0,3},{1,0},{2,1},{3,2},{4,7},{5,4},{6,5},{7,6},{8,11},{9,8},{10,9... | collective-permute-start | bytes 3637256 | tf_op jit(solution)/shard_map/ppermute | solution.py:28
  52.5 46.2 %collective-permute-start.7 = (bf16[296,2048]{1,0:T(8,128)(2,1)S(1)}, bf16[296,2048]{1,0:T(8,128)(2,1)S(1)}, u32[]{:S(2)}, u32[]{:S(2)}) collective-permute-start(bf16[296,2048]{1,0:T(8,128)(2,1)S(1)} %get-tuple-element.81), channel_id=1, source_target_pairs={{0,2},{1,3},{2,0},{3,1},{4,6},{5,7},{6,4},{7,5},{8,10},{9,11},{10,... | collective-permute-start | bytes 3637256 | tf_op jit(solution)/shard_map/ppermute | solution.py:28
  52.6 27.0 %collective-permute-start.11 = (bf16[288,2048]{1,0:T(8,128)(2,1)S(1)}, bf16[288,2048]{1,0:T(8,128)(2,1)S(1)}, u32[]{:S(2)}, u32[]{:S(2)}) collective-permute-start(bf16[288,2048]{1,0:T(8,128)(2,1)S(1)} %get-tuple-element.92), channel_id=1, source_target_pairs={{0,12},{1,13},{2,14},{3,15},{4,0},{5,1},{6,2},{7,3},{8,4},{9,5},{1... | collective-permute-start | bytes 3538952 | tf_op jit(solution)/shard_map/ppermute | solution.py:28
  72.0 27.9 %collective-permute-start.10 = (bf16[288,2048]{1,0:T(8,128)(2,1)S(1)}, bf16[288,2048]{1,0:T(8,128)(2,1)S(1)}, u32[]{:S(2)}, u32[]{:S(2)}) collective-permute-start(bf16[288,2048]{1,0:T(8,128)(2,1)S(1)} %get-tuple-element.90), channel_id=1, source_target_pairs={{0,8},{1,9},{2,10},{3,11},{4,12},{5,13},{6,14},{7,15},{8,0},{9,1},... | collective-permute-start | bytes 3538952 | tf_op jit(solution)/shard_map/ppermute | solution.py:28
  121.0 16.6 %collective-permute-start.18 = (bf16[288,1024]{1,0:T(8,128)(2,1)S(1)}, bf16[288,1024]{1,0:T(8,128)(2,1)S(1)}, u32[]{:S(2)}, u32[]{:S(2)}) collective-permute-start(bf16[288,1024]{1,0:T(8,128)(2,1)S(1)} %get-tuple-element.122), channel_id=1, source_target_pairs={{0,12},{1,13},{2,14},{3,15},{4,0},{5,1},{6,2},{7,3},{8,4},{9,5},{1... | collective-permute-start | bytes 1769480 | tf_op jit(solution)/shard_map/ppermute | solution.py:28
  127.8 22.7 %collective-permute-start.20 = (bf16[288,1024]{1,0:T(8,128)(2,1)S(1)}, bf16[288,1024]{1,0:T(8,128)(2,1)S(1)}, u32[]{:S(2)}, u32[]{:S(2)}) collective-permute-start(bf16[288,1024]{1,0:T(8,128)(2,1)S(1)} %get-tuple-element.126), channel_id=1, source_target_pairs={{0,4},{1,5},{2,6},{3,7},{4,8},{5,9},{6,10},{7,11},{8,12},{9,13},{1... | collective-permute-start | bytes 1769480 | tf_op jit(solution)/shard_map/ppermute | solution.py:28
  127.8 28.4 %collective-permute-start.12 = (bf16[296,1024]{1,0:T(8,128)(2,1)S(1)}, bf16[296,1024]{1,0:T(8,128)(2,1)S(1)}, u32[]{:S(2)}, u32[]{:S(2)}) collective-permute-start(bf16[296,1024]{1,0:T(8,128)(2,1)S(1)} %get-tuple-element.114), channel_id=1, source_target_pairs={{0,3},{1,0},{2,1},{3,2},{4,7},{5,4},{6,5},{7,6},{8,11},{9,8},{10,9... | collective-permute-start | bytes 1818632 | tf_op jit(solution)/shard_map/ppermute | solution.py:28
  129.8 26.4 %collective-permute-start.13 = (bf16[296,1024]{1,0:T(8,128)(2,1)S(1)}, bf16[296,1024]{1,0:T(8,128)(2,1)S(1)}, u32[]{:S(2)}, u32[]{:S(2)}) collective-permute-start(bf16[296,1024]{1,0:T(8,128)(2,1)S(1)} %get-tuple-element.115), channel_id=1, source_target_pairs={{0,2},{1,3},{2,0},{3,1},{4,6},{5,7},{6,4},{7,5},{8,10},{9,11},{10,... | collective-permute-start | bytes 1818632 | tf_op jit(solution)/shard_map/ppermute | solution.py:28
  130.6 28.3 %collective-permute-start.14 = (bf16[296,1024]{1,0:T(8,128)(2,1)S(1)}, bf16[296,1024]{1,0:T(8,128)(2,1)S(1)}, u32[]{:S(2)}, u32[]{:S(2)}) collective-permute-start(bf16[296,1024]{1,0:T(8,128)(2,1)S(1)} %get-tuple-element.116), channel_id=1, source_target_pairs={{0,1},{1,2},{2,3},{3,0},{4,5},{5,6},{6,7},{7,4},{8,9},{9,10},{10,1... | collective-permute-start | bytes 1818632 | tf_op jit(solution)/shard_map/ppermute | solution.py:28
  137.6 12.9 %collective-permute-start.19 = (bf16[288,1024]{1,0:T(8,128)(2,1)S(1)}, bf16[288,1024]{1,0:T(8,128)(2,1)S(1)}, u32[]{:S(2)}, u32[]{:S(2)}) collective-permute-start(bf16[288,1024]{1,0:T(8,128)(2,1)S(1)} %get-tuple-element.125), channel_id=1, source_target_pairs={{0,8},{1,9},{2,10},{3,11},{4,12},{5,13},{6,14},{7,15},{8,0},{9,1},... | collective-permute-start | bytes 1769480 | tf_op jit(solution)/shard_map/ppermute | solution.py:28
  154.5 11.3 %collective-permute-start.21 = (bf16[128,1024]{1,0:T(8,128)(2,1)S(1)}, bf16[128,1024]{1,0:T(8,128)(2,1)S(1)}, u32[]{:S(2)}, u32[]{:S(2)}) collective-permute-start(bf16[128,1024]{1,0:T(8,128)(2,1)S(1)} %get-tuple-element.128), channel_id=1, source_target_pairs={{0,3},{1,0},{2,1},{3,2},{4,7},{5,4},{6,5},{7,6},{8,11},{9,8},{10,9... | collective-permute-start | bytes 786440 | tf_op jit(solution)/shard_map/ppermute | solution.py:28
  164.1 7.0 %collective-permute-start.16 = (bf16[136,1024]{1,0:T(8,128)(2,1)S(1)}, bf16[136,1024]{1,0:T(8,128)(2,1)S(1)}, u32[]{:S(2)}, u32[]{:S(2)}) collective-permute-start(bf16[136,1024]{1,0:T(8,128)(2,1)S(1)} %get-tuple-element.119), channel_id=1, source_target_pairs={{0,8},{1,9},{2,10},{3,11},{4,12},{5,13},{6,14},{7,15},{8,0},{9,1},... | collective-permute-start | bytes 835592 | tf_op jit(solution)/shard_map/ppermute | solution.py:28
  165.8 8.1 %collective-permute-start.17 = (bf16[136,1024]{1,0:T(8,128)(2,1)S(1)}, bf16[136,1024]{1,0:T(8,128)(2,1)S(1)}, u32[]{:S(2)}, u32[]{:S(2)}) collective-permute-start(bf16[136,1024]{1,0:T(8,128)(2,1)S(1)} %get-tuple-element.120), channel_id=1, source_target_pairs={{0,4},{1,5},{2,6},{3,7},{4,8},{5,9},{6,10},{7,11},{8,12},{9,13},{1... | collective-permute-start | bytes 835592 | tf_op jit(solution)/shard_map/ppermute | solution.py:28
  165.8 9.2 %collective-permute-start.23 = (bf16[128,1024]{1,0:T(8,128)(2,1)S(1)}, bf16[128,1024]{1,0:T(8,128)(2,1)S(1)}, u32[]{:S(2)}, u32[]{:S(2)}) collective-permute-start(bf16[128,1024]{1,0:T(8,128)(2,1)S(1)} %get-tuple-element.131), channel_id=1, source_target_pairs={{0,1},{1,2},{2,3},{3,0},{4,5},{5,6},{6,7},{7,4},{8,9},{9,10},{10,1... | collective-permute-start | bytes 786440 | tf_op jit(solution)/shard_map/ppermute | solution.py:28
  165.8 9.2 %collective-permute-start.22 = (bf16[128,1024]{1,0:T(8,128)(2,1)S(1)}, bf16[128,1024]{1,0:T(8,128)(2,1)S(1)}, u32[]{:S(2)}, u32[]{:S(2)}) collective-permute-start(bf16[128,1024]{1,0:T(8,128)(2,1)S(1)} %get-tuple-element.130), channel_id=1, source_target_pairs={{0,2},{1,3},{2,0},{3,1},{4,6},{5,7},{6,4},{7,5},{8,10},{9,11},{10,... | collective-permute-start | bytes 786440 | tf_op jit(solution)/shard_map/ppermute | solution.py:28
  175.7 21.5 %collective-permute-start.24 = (bf16[128,2048]{1,0:T(8,128)(2,1)S(1)}, bf16[128,2048]{1,0:T(8,128)(2,1)S(1)}, u32[]{:S(2)}, u32[]{:S(2)}) collective-permute-start(bf16[128,2048]{1,0:T(8,128)(2,1)S(1)} %get-tuple-element.132), channel_id=1, source_target_pairs={{16,0},{32,16},{48,32},{64,48},{80,64},{96,80},{112,96},{17,1},{33... | collective-permute-start | bytes 1572872 | tf_op jit(solution)/shard_map/ppermute | solution.py:448
  (12 other events, 118.9 us)

commit v3 on v2

--- a/solution.py
+++ b/solution.py
@@ -146,7 +146,7 @@
         ),
         in_specs=[SMEM] + [VMEM] * 8,
         out_specs=(VMEM, VMEM),
-        compiler_params=params(6),
+        compiler_params=params(24),
         cost_estimate=cost(4 * GROUP * tokens * width, 7_000_000),
     )(who, *a, *b)
 
@@ -318,48 +318,60 @@
     )(*b, hg)
 
 
-def gather_kernel(tokens, along_row, who_ref, *refs):
-    id_refs, back_refs, outs = refs[:4], refs[4:8], refs[8:]
-    half = back_refs[0].shape[1]
+def places_kernel(tokens, along_row, who_ref, *refs):
+    id_refs, out = refs[:4], refs[4]
     ids = [r[tokens : tokens + META, 0:tokens].astype(F32) for r in id_refs]
     pairs = [(near, far) for near in range(SIDE) for far in range(SIDE)]
     me = who_ref[0]
     experts = [as_float(ahead(me, 0, f) if along_row else ahead(me, f, 0)) for f in range(SIDE)]
     slot = slots([ids[n] for n, _ in pairs], [experts[f] for _, f in pairs])
     for near in range(SIDE):
-        places = []
-        for far in range(SIDE):
-            spread = one_hot(slot[near * SIDE + far], GROUP, near * CAP)
-            places.append(spread.T.astype(BF16))
-        for left in range(0, half, 512):
-            cols = slice(left, left + 512)
-            part = jnp.dot(places[0], back_refs[0][0:GROUP, cols], preferred_element_type=F32)
-            for far in range(1, SIDE):
-                part += jnp.dot(
-                    places[far], back_refs[far][0:GROUP, cols], preferred_element_type=F32
-                )
+        spread = [one_hot(slot[near * SIDE + far], GROUP, near * CAP) for far in range(SIDE)]
+        out[near * tokens : (near + 1) * tokens] = jnp.concatenate(spread, axis=0).T.astype(BF16)
+
+
+def places(who, blocks, tokens, along_row):
+    return pl.pallas_call(
+        functools.partial(places_kernel, tokens, along_row),
+        out_shape=jax.ShapeDtypeStruct((SIDE * tokens, SIDE * GROUP), BF16),
+        in_specs=[SMEM] + [VMEM] * 4,
+        out_specs=VMEM,
+        compiler_params=params(6),
+        cost_estimate=cost(0, 4_000_000),
+    )(who, *blocks)
+
+
+def gather_kernel(tokens, along_row, places_ref, *refs):
+    back_refs, outs = refs[:4], refs[4:]
+    half = back_refs[0].shape[1]
+    for left in range(0, half, 512):
+        cols = slice(left, left + 512)
+        rows = jnp.concatenate([r[0:GROUP, cols] for r in back_refs], axis=0)
+        for near in range(SIDE):
+            mine = places_ref[near * tokens : (near + 1) * tokens]
+            part = jnp.dot(mine, rows, preferred_element_type=F32)
             outs[near][0:tokens, cols] = part.astype(BF16)
-        if along_row:
-            lines = [
-                r[GROUP : GROUP + META, 0:tokens].astype(F32)[near : near + 1] for r in back_refs
-            ]
+    if along_row:
+        tables = [r[GROUP : GROUP + META, 0:tokens].astype(F32) for r in back_refs]
+        for near in range(SIDE):
+            lines = [t[near : near + 1] for t in tables]
             lines.append(jnp.zeros((META - SIDE, tokens), F32))
             table = jnp.concatenate(lines, axis=0)
             table = jnp.concatenate([table, jnp.zeros((META, half - tokens), F32)], axis=1)
             outs[near][tokens : tokens + META] = table.astype(BF16)
 
 
-def gather(who, blocks, back, tokens, along_row):
+def gather(spots, back, tokens, along_row):
     half = back[0].shape[1]
     rows = tokens + META if along_row else tokens
     return pl.pallas_call(
         functools.partial(gather_kernel, tokens, along_row),
         out_shape=[jax.ShapeDtypeStruct((rows, half), BF16)] * SIDE,
-        in_specs=[SMEM] + [VMEM] * 8,
+        in_specs=[VMEM] * 5,
         out_specs=[VMEM] * SIDE,
         compiler_params=params(8),
         cost_estimate=cost(32 * tokens * GROUP * half, 6_000_000),
-    )(who, *blocks, *back)
+    )(spots, *back)
 
 
 def finish_kernel(tokens, who_ref, g_ref, ids_ref, *refs):
@@ -396,13 +408,17 @@
     )(who, g, ids, *firsts, *seconds)
 
 
-def exchange(one, two, one_route, two_route, meanwhile=lambda: ()):
+def exchange(one, two, one_route, two_route, rounds, meanwhile=lambda: ()):
     one, two = list(one), list(two)
-    for d in (1, 3, 2):
+    for d in (1, 3):
         one[d] = shift(one[d], *one_route(d))
-    for d in (1, 3):
         two[d] = shift(two[d], *two_route(d))
-    two[2] = shift(after(two[2], two[1], *meanwhile()), *two_route(2))
+    done = meanwhile()
+    if rounds:
+        one[2], two[2] = after(one[2], one[1], one[3], *done), after(two[2], two[1], two[3], *done)
+    else:
+        two[2] = after(two[2], two[1], *done)
+    one[2], two[2] = shift(one[2], *one_route(2)), shift(two[2], *two_route(2))
     return one, two
 
 
@@ -415,7 +431,7 @@
     a0, b0 = pack(x, g, ids, gates)
     wg, wu, wd = gate_weight[0, 0], up_weight[0, 0], down_weight[0, 0]
     wdt, wut = after(wd, a0).T, after(wu, a0).T
-    a, b = exchange([a0] * SIDE, [b0] * SIDE, lambda d: (d, 0), lambda d: (0, d), lambda: (wdt,))
+    a, b = exchange([a0] * SIDE, [b0] * SIDE, lambda d: (d, 0), lambda d: (0, d), False, lambda: (wdt,))
     wgt = after(wg, wut).T
 
     send_a, send_b, turn = [None] * SIDE, [None] * SIDE, after(who, wgt)
@@ -424,8 +440,10 @@
         turn = after(who, send_a[d])
     own = ready(who, send_a[0], send_b[0], wg, wu, wdt, tokens)
     rows_in, rows_grad = exchange(
-        send_a, send_b, lambda d: (0, d), lambda d: (d, 0), lambda: own[-1:]
+        send_a, send_b, lambda d: (0, d), lambda d: (d, 0), True, lambda: own[-1:]
     )
+    row_spots = places(after(who, own[-1]), a, tokens, True)
+    col_spots = places(after(who, row_spots), b, tokens, False)
 
     made = [own]
     for d in (1, 2, 3):
@@ -434,14 +452,13 @@
     gg, gu, hg = made[:3]
     down_wgrad = down_wgrads(rows_grad, hg)
     first, second = exchange(
-        made[3:7], made[7:11], lambda d: (0, -d), lambda d: (-d, 0), lambda: (down_wgrad,)
+        made[3:7], made[7:11], lambda d: (0, -d), lambda d: (-d, 0), False, lambda: (down_wgrad,)
     )
     gate_wgrad, up_wgrad = up_wgrads(rows_in, gg, gu)
 
-    turn = after(who, gate_wgrad)
-    first = gather(turn, a, first, tokens, True)
-    second = gather(turn, b, second, tokens, False)
-    first, second = exchange(first, second, lambda d: (-d, 0), lambda d: (0, -d))
+    first = gather(after(row_spots, gate_wgrad), first, tokens, True)
+    second = gather(after(col_spots, gate_wgrad), second, tokens, False)
+    first, second = exchange(first, second, lambda d: (-d, 0), lambda d: (0, -d), False)
     section_grad, gate_grad = finish(who, g, ids, first, second)
 
     sections = lax.axis_size("section")

time: 202 us -> 185 us (0.916); the launches traced: 198 us -> 184 us
  starting transfers between devices: 47.1 us -> 29.1 us
  waiting for transfers between devices: 64.9 us -> 79.5 us
  Pallas kernels: 70 us -> 59.8 us
    ppermute x24, waiting for transfers between devices: 57 us -> 71.4 us  [shift(): return lax.ppermute(block, 'expert', route)]
    ppermute x1, starting transfers between devices: 13.6 us -> 2.39 us  [local(): lax.ppermute(section_grad, 'section', [(i + 1, i) for i in range(sections...]
    pallas_call x1, Pallas kernels: 18.1 us -> 8.7 us  [middle(): pl.pallas_call(functools.partial(middle_kernel, tokens), out_shape=[jax.S...]
    ppermute x24, starting transfers between devices: 33.5 us -> 26.7 us  [shift(): return lax.ppermute(block, 'expert', route)]
    pallas_call x2, Pallas kernels: 7.98 us -> 3.08 us  [gather(): pl.pallas_call(functools.partial(gather_kernel, tokens, along_row), out_s...]
    pallas_call x0 -> x2, Pallas kernels: none -> 3.92 us  [places(): pl.pallas_call(functools.partial(places_kernel, tokens, along_row), out_s...]
  transfers between devices with their start and end apart: 25 -> 25, of which waited for: 13 -> 12; matrix products, arithmetic and copies ran while one was open for 6% -> 7% of each run, Pallas kernels for 22% -> 23%
where the time goes in v3:
time: 185 us; the launch traced here: 184 us
  waiting for transfers between devices  79.5 us (43%)
  Pallas kernels  59.8 us (32%)
  starting transfers between devices  29.1 us (16%)
  local copies, waits for them, and re-layouts  15.2 us (8%)
    ppermute x24, waiting for transfers between devices, shift(): return lax.ppermute(block, 'expert', route)  71.4 us
    ppermute x24, starting transfers between devices, shift(): return lax.ppermute(block, 'expert', route)  26.7 us
    unnamed x26, local copies, waits for them, and re-layouts  15.2 us
    pallas_call x4, Pallas kernels, ready(): pl.pallas_call(functools.partial(ready_kernel, tokens), out_shape=(wide,...  11.9 us
    pallas_call x4, Pallas kernels, select(): pl.pallas_call(functools.partial(select_kernel, tokens, step), out_shape=...  11.8 us
    pallas_call x1, Pallas kernels, up_wgrads(): pl.pallas_call(up_wgrad_kernel, grid=(width // tile,), out_shape=[jax.Sha...  11.3 us
    pallas_call x1, Pallas kernels, middle(): pl.pallas_call(functools.partial(middle_kernel, tokens), out_shape=[jax.S...  8.7 us
    ppermute x1, waiting for transfers between devices, local(): lax.ppermute(section_grad, 'section', [(i + 1, i) for i in range(sections...  8.09 us
  transfers between devices with their start and end apart: 25, of which 12 were waited for; matrix products, arithmetic and copies ran while one was open for 7% of the time, Pallas kernels for 23%

profile of v3, /device:TPU:1, one launch (start us, length us, event | category | flops | bytes accessed | tf_op | source)
XLA Modules:
  0.0 184.4 jit_solution(16525883958967013562)
XLA Ops:
  7.6 2.7 %collective-permute-start.2 = (bf16[136,2048]{1,0:T(8,128)(2,1)}, bf16[136,2048]{1,0:T(8,128)(2,1)}, u32[]{:S(2)}, u32[]{:S(2)}) collective-permute-start(bf16[136,2048]{1,0:T(8,128)(2,1)} %get-tuple-element.74.refs_0_), channel_id=1, source_target_pairs={{0,12},{1,13},{2,14},{3,15},{4,0},{5,1},{6,2},{7,3},{8,4},{9,5},{1... | collective-permute-start | bytes 1671176 | tf_op jit(solution)/shard_map/ppermute | solution.py:28
  11.4 4.8 %copy.14 = bf16[1,1,768,2048]{2,3,1,0:T(8,128)(2,1)} copy(bf16[1,1,768,2048]{3,2,1,0:T(8,128)(2,1)} %param.13) | data formatting | bytes 6291456 | tf_op args[6]
  16.2 4.0 %collective-permute-done.3.refs_5_.refs_1_ = bf16[136,2048]{1,0:T(8,128)(2,1)} collective-permute-done((bf16[136,2048]{1,0:T(8,128)(2,1)}, bf16[136,2048]{1,0:T(8,128)(2,1)}, u32[]{:S(2)}, u32[]{:S(2)}) %collective-permute-start.3) | collective-permute-done | bytes 557088 | tf_op jit(solution)/shard_map/ppermute | solution.py:28
  21.2 2.9 %copy.12 = bf16[1,1,2048,768]{2,3,1,0:T(8,128)(2,1)} copy(bf16[1,1,2048,768]{3,2,1,0:T(8,128)(2,1)S(1)} %copy-done) | data formatting | bytes 6291456 | tf_op args[4]
  24.1 4.6 %copy.13 = bf16[1,1,2048,768]{2,3,1,0:T(8,128)(2,1)} copy(bf16[1,1,2048,768]{3,2,1,0:T(8,128)(2,1)} %param.12) | data formatting | bytes 6291456 | tf_op args[5]
  28.7 10.0 %collective-permute-done.refs_1_ = bf16[136,2048]{1,0:T(8,128)(2,1)} collective-permute-done((bf16[136,2048]{1,0:T(8,128)(2,1)}, bf16[136,2048]{1,0:T(8,128)(2,1)}, u32[]{:S(2)}, u32[]{:S(2)}) %collective-permute-start) | collective-permute-done | bytes 557088 | tf_op jit(solution)/shard_map/ppermute | solution.py:28
  40.8 2.9 %shard_map.111 = (bf16[296,2048]{1,0:T(8,128)(2,1)S(1)}, bf16[288,2048]{1,0:T(8,128)(2,1)S(1)}) custom-call(s32[1]{0:T(128)} %bitcast.who_ref, bf16[136,2048]{1,0:T(8,128)(2,1)S(1)} %copy-done.5, bf16[136,2048]{1,0:T(8,128)(2,1)} %collective-permute-done.refs_1_, bf16[136,2048]{1,0:T(8,128)(2,1)} %collective-permute-done.1.refs_2_, ...), custom_call_target="tpu_custom_call" | custom-call | flops 301989888 | bytes 7000000 | tf_op jit(solution)/shard_map/pallas_call | solution.py:141
  43.8 2.9 %shard_map.112 = (bf16[296,2048]{1,0:T(8,128)(2,1)S(1)}, bf16[288,2048]{1,0:T(8,128)(2,1)S(1)}) custom-call(s32[1]{0:T(128)} %bitcast.who_ref, bf16[136,2048]{1,0:T(8,128)(2,1)S(1)} %copy-done.5, bf16[136,2048]{1,0:T(8,128)(2,1)} %collective-permute-done.refs_1_, bf16[136,2048]{1,0:T(8,128)(2,1)} %collective-permute-done.1.refs_2_, ...), custom_call_target="tpu_custom_call" | custom-call | flops 301989888 | bytes 7000000 | tf_op jit(solution)/shard_map/pallas_call | solution.py:141
  52.1 3.0 %shard_map.113 = (bf16[296,2048]{1,0:T(8,128)(2,1)S(1)}, bf16[288,2048]{1,0:T(8,128)(2,1)S(1)}) custom-call(s32[1]{0:T(128)} %bitcast.who_ref, bf16[136,2048]{1,0:T(8,128)(2,1)S(1)} %copy-done.6, bf16[136,2048]{1,0:T(8,128)(2,1)} %collective-permute-done.refs_1_, bf16[136,2048]{1,0:T(8,128)(2,1)} %collective-permute-done.1.refs_2_, ...), custom_call_target="tpu_custom_call" | custom-call | flops 301989888 | bytes 7000000 | tf_op jit(solution)/shard_map/pallas_call | solution.py:141
  55.1 3.0 %shard_map.114 = (bf16[296,2048]{1,0:T(8,128)(2,1)S(1)}, bf16[288,2048]{1,0:T(8,128)(2,1)S(1)}) custom-call(s32[1]{0:T(128)} %bitcast.who_ref, bf16[136,2048]{1,0:T(8,128)(2,1)S(1)} %copy-done.6, bf16[136,2048]{1,0:T(8,128)(2,1)} %collective-permute-done.refs_1_, bf16[136,2048]{1,0:T(8,128)(2,1)} %collective-permute-done.1.refs_2_, ...), custom_call_target="tpu_custom_call" | custom-call | flops 301989888 | bytes 7000000 | tf_op jit(solution)/shard_map/pallas_call | solution.py:141
  58.1 3.0 %shard_map.115 = (f32[288,768]{1,0:T(8,128)S(1)}, f32[288,768]{1,0:T(8,128)S(1)}, f32[288,768]{1,0:T(8,128)S(1)}, f32[288,128]{1,0:T(8,128)S(1)}, f32[8,128]{1,0:T(8,128)S(1)}) custom-call(s32[1]{0:T(128)} %bitcast.who_ref, bf16[296,2048]{1,0:T(8,128)(2,1)S(1)} %get-tuple-element.87.a_ref.refs_0_, bf16[288,2048]{1,0:T(8,128)(2,1)S(1)} %get-tuple-element.88.b_ref.refs_0_, ...), custom_call_target="tpu_custom_call" | custom-call | flops 2717908992 | bytes 6000000 | tf_op jit(solution)/shard_map/pallas_call | solution.py:182
  61.1 11.6 %collective-permute-done.6.a_ref.refs_1_ = bf16[296,2048]{1,0:T(8,128)(2,1)S(1)} collective-permute-done((bf16[296,2048]{1,0:T(8,128)(2,1)S(1)}, bf16[296,2048]{1,0:T(8,128)(2,1)S(1)}, u32[]{:S(2)}, u32[]{:S(2)}) %collective-permute-start.6) | collective-permute-done | bytes 1212448 | tf_op jit(solution)/shard_map/ppermute | solution.py:28
  78.2 3.0 %shard_map.119 = (f32[288,768]{1,0:T(8,128)S(1)}, f32[288,768]{1,0:T(8,128)S(1)}, f32[288,768]{1,0:T(8,128)S(1)}, f32[288,128]{1,0:T(8,128)S(1)}, f32[8,128]{1,0:T(8,128)S(1)}) custom-call(s32[1]{0:T(128)} %bitcast.who_ref, bf16[296,2048]{1,0:T(8,128)(2,1)S(1)} %collective-permute-done.7.a_ref.refs_3_, ...), custom_call_target="tpu_custom_call" | custom-call | flops 2717908992 | bytes 6000000 | tf_op jit(solution)/shard_map/pallas_call | solution.py:182
  81.2 3.0 %shard_map.117 = (f32[288,768]{1,0:T(8,128)S(1)}, f32[288,768]{1,0:T(8,128)S(1)}, f32[288,768]{1,0:T(8,128)S(1)}, f32[288,128]{1,0:T(8,128)S(1)}, f32[8,128]{1,0:T(8,128)S(1)}) custom-call(s32[1]{0:T(128)} %bitcast.who_ref, bf16[296,2048]{1,0:T(8,128)(2,1)S(1)} %collective-permute-done.6.a_ref.refs_1_, ...), custom_call_target="tpu_custom_call" | custom-call | flops 2717908992 | bytes 6000000 | tf_op jit(solution)/shard_map/pallas_call | solution.py:182
  84.2 19.8 %collective-permute-done.11.b_ref.refs_2_ = bf16[288,2048]{1,0:T(8,128)(2,1)S(1)} collective-permute-done((bf16[288,2048]{1,0:T(8,128)(2,1)S(1)}, bf16[288,2048]{1,0:T(8,128)(2,1)S(1)}, u32[]{:S(2)}, u32[]{:S(2)}) %collective-permute-start.11) | collective-permute-done | bytes 1179680 | tf_op jit(solution)/shard_map/ppermute | solution.py:28
  104.0 3.0 %shard_map.118 = (f32[288,768]{1,0:T(8,128)S(1)}, f32[288,768]{1,0:T(8,128)S(1)}, f32[288,768]{1,0:T(8,128)S(1)}, f32[288,128]{1,0:T(8,128)S(1)}, f32[8,128]{1,0:T(8,128)S(1)}) custom-call(s32[1]{0:T(128)} %bitcast.who_ref, bf16[296,2048]{1,0:T(8,128)(2,1)S(1)} %collective-permute-done.8.a_ref.refs_2_, ...), custom_call_target="tpu_custom_call" | custom-call | flops 2717908992 | bytes 6000000 | tf_op jit(solution)/shard_map/pallas_call | solution.py:182
  107.0 8.7 %shard_map.120 = (bf16[1152,768]{1,0:T(8,128)(2,1)S(1)}, bf16[1152,768]{1,0:T(8,128)(2,1)S(1)}, bf16[1152,768]{1,0:T(8,128)(2,1)S(1)}, bf16[296,1024]{1,0:T(8,12...) custom-call(f32[288,768]{1,0:T(8,128)S(1)} %get-tuple-element.92.ref, ...), custom_call_target="tpu_custom_call" | custom-call | flops 7247757312 | bytes 10000000 | tf_op jit(solution)/shard_map/pallas_call | solution.py:255
  124.6 6.1 %shard_map.124 = bf16[768,2048]{1,0:T(8,128)(2,1)} custom-call(bf16[288,2048]{1,0:T(8,128)(2,1)S(1)} %get-tuple-element.88.b_ref.refs_0_, bf16[288,2048]{1,0:T(8,128)(2,1)S(1)} %collective-permute-done.9.b_ref.refs_1_, bf16[288,2048]{1,0:T(8,128)(2,1)S(1)} %collective-permute-done.11.b_ref.refs_2_, ...), custom_call_target="tpu_custom_call" | custom-call | flops 3623878656 | bytes 10000000 | tf_op jit(solution)/shard_map/pallas_call | solution.py:309
  130.8 11.3 %shard_map.121 = (bf16[2048,768]{1,0:T(8,128)(2,1)}, bf16[2048,768]{1,0:T(8,128)(2,1)}) custom-call(bf16[296,2048]{1,0:T(8,128)(2,1)S(1)} %get-tuple-element.87.a_ref.refs_0_, bf16[296,2048]{1,0:T(8,128)(2,1)S(1)} %collective-permute-done.6.a_ref.refs_1_, bf16[296,2048]{1,0:T(8,128)(2,1)S(1)} %collective-permute-done.8.a_ref.refs_2_, ...), custom_call_target="tpu_custom_call" | custom-call | flops 7247757312 | bytes 15000000 | tf_op jit(solution)/shard_map/pallas_call | solution.py:288
  142.1 5.0 %collective-permute-done.19.refs_2_ = bf16[288,1024]{1,0:T(8,128)(2,1)S(1)} collective-permute-done((bf16[288,1024]{1,0:T(8,128)(2,1)S(1)}, bf16[288,1024]{1,0:T(8,128)(2,1)S(1)}, u32[]{:S(2)}, u32[]{:S(2)}) %collective-permute-start.19) | collective-permute-done | bytes 589856 | tf_op jit(solution)/shard_map/ppermute | solution.py:28
  148.7 4.6 %collective-permute-done.14.refs_3_ = bf16[296,1024]{1,0:T(8,128)(2,1)S(1)} collective-permute-done((bf16[296,1024]{1,0:T(8,128)(2,1)S(1)}, bf16[296,1024]{1,0:T(8,128)(2,1)S(1)}, u32[]{:S(2)}, u32[]{:S(2)}) %collective-permute-start.14) | collective-permute-done | bytes 606240 | tf_op jit(solution)/shard_map/ppermute | solution.py:28
  158.3 4.4 %collective-permute-done.15.refs_1_ = bf16[136,1024]{1,0:T(8,128)(2,1)S(1)} collective-permute-done((bf16[136,1024]{1,0:T(8,128)(2,1)S(1)}, bf16[136,1024]{1,0:T(8,128)(2,1)S(1)}, u32[]{:S(2)}, u32[]{:S(2)}) %collective-permute-start.15) | collective-permute-done | bytes 278560 | tf_op jit(solution)/shard_map/ppermute | solution.py:28
  165.4 7.1 %collective-permute-done.17.refs_3_ = bf16[136,1024]{1,0:T(8,128)(2,1)S(1)} collective-permute-done((bf16[136,1024]{1,0:T(8,128)(2,1)S(1)}, bf16[136,1024]{1,0:T(8,128)(2,1)S(1)}, u32[]{:S(2)}, u32[]{:S(2)}) %collective-permute-start.17) | collective-permute-done | bytes 278560 | tf_op jit(solution)/shard_map/ppermute | solution.py:28
  175.5 8.1 %collective-permute-done.24 = bf16[128,2048]{1,0:T(8,128)(2,1)S(1)} collective-permute-done((bf16[128,2048]{1,0:T(8,128)(2,1)S(1)}, bf16[128,2048]{1,0:T(8,128)(2,1)S(1)}, u32[]{:S(2)}, u32[]{:S(2)}) %collective-permute-start.24) | collective-permute-done | bytes 524320 | tf_op jit(solution)/shard_map/ppermute | solution.py:465
  (69 shorter events, 44.1 us)
Async XLA Ops:
  2.9 17.3 %collective-permute-start.3 = (bf16[136,2048]{1,0:T(8,128)(2,1)}, bf16[136,2048]{1,0:T(8,128)(2,1)}, u32[]{:S(2)}, u32[]{:S(2)}) collective-permute-start(bf16[136,2048]{1,0:T(8,128)(2,1)} %get-tuple-element.80.refs_4_.refs_0_), channel_id=1, source_target_pairs={{0,1},{1,2},{2,3},{3,0},{4,5},{5,6},{6,7},{7,4},{8,9},{9,10},{10,1... | collective-permute-start | bytes 1671176 | tf_op jit(solution)/shard_map/ppermute | solution.py:28
  5.4 23.3 %collective-permute-start.5 = (bf16[136,2048]{1,0:T(8,128)(2,1)}, bf16[136,2048]{1,0:T(8,128)(2,1)}, u32[]{:S(2)}, u32[]{:S(2)}) collective-permute-start(bf16[136,2048]{1,0:T(8,128)(2,1)} %get-tuple-element.80.refs_4_.refs_0_), channel_id=1, source_target_pairs={{0,3},{1,0},{2,1},{3,2},{4,7},{5,4},{6,5},{7,6},{8,11},{9,8},{10,9... | collective-permute-start | bytes 1671176 | tf_op jit(solution)/shard_map/ppermute | solution.py:28
  7.6 21.1 %collective-permute-start.2 = (bf16[136,2048]{1,0:T(8,128)(2,1)}, bf16[136,2048]{1,0:T(8,128)(2,1)}, u32[]{:S(2)}, u32[]{:S(2)}) collective-permute-start(bf16[136,2048]{1,0:T(8,128)(2,1)} %get-tuple-element.74.refs_0_), channel_id=1, source_target_pairs={{0,12},{1,13},{2,14},{3,15},{4,0},{5,1},{6,2},{7,3},{8,4},{9,5},{1... | collective-permute-start | bytes 1671176 | tf_op jit(solution)/shard_map/ppermute | solution.py:28
  10.4 18.3 %collective-permute-start.1 = (bf16[136,2048]{1,0:T(8,128)(2,1)}, bf16[136,2048]{1,0:T(8,128)(2,1)}, u32[]{:S(2)}, u32[]{:S(2)}) collective-permute-start(bf16[136,2048]{1,0:T(8,128)(2,1)} %get-tuple-element.74.refs_0_), channel_id=1, source_target_pairs={{0,8},{1,9},{2,10},{3,11},{4,12},{5,13},{6,14},{7,15},{8,0},{9,1},... | collective-permute-start | bytes 1671176 | tf_op jit(solution)/shard_map/ppermute | solution.py:28
  10.7 28.0 %collective-permute-start = (bf16[136,2048]{1,0:T(8,128)(2,1)}, bf16[136,2048]{1,0:T(8,128)(2,1)}, u32[]{:S(2)}, u32[]{:S(2)}) collective-permute-start(bf16[136,2048]{1,0:T(8,128)(2,1)} %get-tuple-element.74.refs_0_), channel_id=1, source_target_pairs={{0,4},{1,5},{2,6},{3,7},{4,8},{5,9},{6,10},{7,11},{8,12},{9,13},{1... | collective-permute-start | bytes 1671176 | tf_op jit(solution)/shard_map/ppermute | solution.py:28
  20.2 18.5 %collective-permute-start.4 = (bf16[136,2048]{1,0:T(8,128)(2,1)}, bf16[136,2048]{1,0:T(8,128)(2,1)}, u32[]{:S(2)}, u32[]{:S(2)}) collective-permute-start(bf16[136,2048]{1,0:T(8,128)(2,1)} %get-tuple-element.80.refs_4_.refs_0_), channel_id=1, source_target_pairs={{0,2},{1,3},{2,0},{3,1},{4,6},{5,7},{6,4},{7,5},{8,10},{9,11},{10,... | collective-permute-start | bytes 1671176 | tf_op jit(solution)/shard_map/ppermute | solution.py:28
  43.7 29.0 %collective-permute-start.6 = (bf16[296,2048]{1,0:T(8,128)(2,1)S(1)}, bf16[296,2048]{1,0:T(8,128)(2,1)S(1)}, u32[]{:S(2)}, u32[]{:S(2)}) collective-permute-start(bf16[296,2048]{1,0:T(8,128)(2,1)S(1)} %get-tuple-element.81), channel_id=1, source_target_pairs={{0,1},{1,2},{2,3},{3,0},{4,5},{5,6},{6,7},{7,4},{8,9},{9,10},{10,1... | collective-permute-start | bytes 3637256 | tf_op jit(solution)/shard_map/ppermute | solution.py:28
  46.7 27.9 %collective-permute-start.7 = (bf16[296,2048]{1,0:T(8,128)(2,1)S(1)}, bf16[296,2048]{1,0:T(8,128)(2,1)S(1)}, u32[]{:S(2)}, u32[]{:S(2)}) collective-permute-start(bf16[296,2048]{1,0:T(8,128)(2,1)S(1)} %get-tuple-element.83), channel_id=1, source_target_pairs={{0,3},{1,0},{2,1},{3,2},{4,7},{5,4},{6,5},{7,6},{8,11},{9,8},{10,9... | collective-permute-start | bytes 3637256 | tf_op jit(solution)/shard_map/ppermute | solution.py:28
  49.4 27.6 %collective-permute-start.9 = (bf16[288,2048]{1,0:T(8,128)(2,1)S(1)}, bf16[288,2048]{1,0:T(8,128)(2,1)S(1)}, u32[]{:S(2)}, u32[]{:S(2)}) collective-permute-start(bf16[288,2048]{1,0:T(8,128)(2,1)S(1)} %get-tuple-element.93), channel_id=1, source_target_pairs={{0,4},{1,5},{2,6},{3,7},{4,8},{5,9},{6,10},{7,11},{8,12},{9,13},{1... | collective-permute-start | bytes 3538952 | tf_op jit(solution)/shard_map/ppermute | solution.py:28
  49.4 27.6 %collective-permute-start.10 = (bf16[288,2048]{1,0:T(8,128)(2,1)S(1)}, bf16[288,2048]{1,0:T(8,128)(2,1)S(1)}, u32[]{:S(2)}, u32[]{:S(2)}) collective-permute-start(bf16[288,2048]{1,0:T(8,128)(2,1)S(1)} %get-tuple-element.96), channel_id=1, source_target_pairs={{0,12},{1,13},{2,14},{3,15},{4,0},{5,1},{6,2},{7,3},{8,4},{9,5},{1... | collective-permute-start | bytes 3538952 | tf_op jit(solution)/shard_map/ppermute | solution.py:28
  74.6 29.4 %collective-permute-start.8 = (bf16[296,2048]{1,0:T(8,128)(2,1)S(1)}, bf16[296,2048]{1,0:T(8,128)(2,1)S(1)}, u32[]{:S(2)}, u32[]{:S(2)}) collective-permute-start(bf16[296,2048]{1,0:T(8,128)(2,1)S(1)} %get-tuple-element.91), channel_id=1, source_target_pairs={{0,2},{1,3},{2,0},{3,1},{4,6},{5,7},{6,4},{7,5},{8,10},{9,11},{10,... | collective-permute-start | bytes 3637256 | tf_op jit(solution)/shard_map/ppermute | solution.py:28
  77.0 27.0 %collective-permute-start.11 = (bf16[288,2048]{1,0:T(8,128)(2,1)S(1)}, bf16[288,2048]{1,0:T(8,128)(2,1)S(1)}, u32[]{:S(2)}, u32[]{:S(2)}) collective-permute-start(bf16[288,2048]{1,0:T(8,128)(2,1)S(1)} %get-tuple-element.97), channel_id=1, source_target_pairs={{0,8},{1,9},{2,10},{3,11},{4,12},{5,13},{6,14},{7,15},{8,0},{9,1},... | collective-permute-start | bytes 3538952 | tf_op jit(solution)/shard_map/ppermute | solution.py:28
  115.7 15.1 %collective-permute-start.18 = (bf16[288,1024]{1,0:T(8,128)(2,1)S(1)}, bf16[288,1024]{1,0:T(8,128)(2,1)S(1)}, u32[]{:S(2)}, u32[]{:S(2)}) collective-permute-start(bf16[288,1024]{1,0:T(8,128)(2,1)S(1)} %get-tuple-element.130), channel_id=1, source_target_pairs={{0,12},{1,13},{2,14},{3,15},{4,0},{5,1},{6,2},{7,3},{8,4},{9,5},{1... | collective-permute-start | bytes 1769480 | tf_op jit(solution)/shard_map/ppermute | solution.py:28
  121.8 20.3 %collective-permute-start.20 = (bf16[288,1024]{1,0:T(8,128)(2,1)S(1)}, bf16[288,1024]{1,0:T(8,128)(2,1)S(1)}, u32[]{:S(2)}, u32[]{:S(2)}) collective-permute-start(bf16[288,1024]{1,0:T(8,128)(2,1)S(1)} %get-tuple-element.134), channel_id=1, source_target_pairs={{0,4},{1,5},{2,6},{3,7},{4,8},{5,9},{6,10},{7,11},{8,12},{9,13},{1... | collective-permute-start | bytes 1769480 | tf_op jit(solution)/shard_map/ppermute | solution.py:28
  121.9 26.8 %collective-permute-start.12 = (bf16[296,1024]{1,0:T(8,128)(2,1)S(1)}, bf16[296,1024]{1,0:T(8,128)(2,1)S(1)}, u32[]{:S(2)}, u32[]{:S(2)}) collective-permute-start(bf16[296,1024]{1,0:T(8,128)(2,1)S(1)} %get-tuple-element.120), channel_id=1, source_target_pairs={{0,3},{1,0},{2,1},{3,2},{4,7},{5,4},{6,5},{7,6},{8,11},{9,8},{10,9... | collective-permute-start | bytes 1818632 | tf_op jit(solution)/shard_map/ppermute | solution.py:28
  123.3 25.5 %collective-permute-start.13 = (bf16[296,1024]{1,0:T(8,128)(2,1)S(1)}, bf16[296,1024]{1,0:T(8,128)(2,1)S(1)}, u32[]{:S(2)}, u32[]{:S(2)}) collective-permute-start(bf16[296,1024]{1,0:T(8,128)(2,1)S(1)} %get-tuple-element.121), channel_id=1, source_target_pairs={{0,2},{1,3},{2,0},{3,1},{4,6},{5,7},{6,4},{7,5},{8,10},{9,11},{10,... | collective-permute-start | bytes 1818632 | tf_op jit(solution)/shard_map/ppermute | solution.py:28
  124.6 28.7 %collective-permute-start.14 = (bf16[296,1024]{1,0:T(8,128)(2,1)S(1)}, bf16[296,1024]{1,0:T(8,128)(2,1)S(1)}, u32[]{:S(2)}, u32[]{:S(2)}) collective-permute-start(bf16[296,1024]{1,0:T(8,128)(2,1)S(1)} %get-tuple-element.122), channel_id=1, source_target_pairs={{0,1},{1,2},{2,3},{3,0},{4,5},{5,6},{6,7},{7,4},{8,9},{9,10},{10,1... | collective-permute-start | bytes 1818632 | tf_op jit(solution)/shard_map/ppermute | solution.py:28
  130.8 16.3 %collective-permute-start.19 = (bf16[288,1024]{1,0:T(8,128)(2,1)S(1)}, bf16[288,1024]{1,0:T(8,128)(2,1)S(1)}, u32[]{:S(2)}, u32[]{:S(2)}) collective-permute-start(bf16[288,1024]{1,0:T(8,128)(2,1)S(1)} %get-tuple-element.133), channel_id=1, source_target_pairs={{0,8},{1,9},{2,10},{3,11},{4,12},{5,13},{6,14},{7,15},{8,0},{9,1},... | collective-permute-start | bytes 1769480 | tf_op jit(solution)/shard_map/ppermute | solution.py:28
  148.6 8.5 %collective-permute-start.21 = (bf16[128,1024]{1,0:T(8,128)(2,1)S(1)}, bf16[128,1024]{1,0:T(8,128)(2,1)S(1)}, u32[]{:S(2)}, u32[]{:S(2)}) collective-permute-start(bf16[128,1024]{1,0:T(8,128)(2,1)S(1)} %get-tuple-element.136), channel_id=1, source_target_pairs={{0,3},{1,0},{2,1},{3,2},{4,7},{5,4},{6,5},{7,6},{8,11},{9,8},{10,9... | collective-permute-start | bytes 786440 | tf_op jit(solution)/shard_map/ppermute | solution.py:28
  156.5 9.0 %collective-permute-start.16 = (bf16[136,1024]{1,0:T(8,128)(2,1)S(1)}, bf16[136,1024]{1,0:T(8,128)(2,1)S(1)}, u32[]{:S(2)}, u32[]{:S(2)}) collective-permute-start(bf16[136,1024]{1,0:T(8,128)(2,1)S(1)} %get-tuple-element.125), channel_id=1, source_target_pairs={{0,8},{1,9},{2,10},{3,11},{4,12},{5,13},{6,14},{7,15},{8,0},{9,1},... | collective-permute-start | bytes 835592 | tf_op jit(solution)/shard_map/ppermute | solution.py:28
  156.8 15.7 %collective-permute-start.17 = (bf16[136,1024]{1,0:T(8,128)(2,1)S(1)}, bf16[136,1024]{1,0:T(8,128)(2,1)S(1)}, u32[]{:S(2)}, u32[]{:S(2)}) collective-permute-start(bf16[136,1024]{1,0:T(8,128)(2,1)S(1)} %get-tuple-element.126), channel_id=1, source_target_pairs={{0,4},{1,5},{2,6},{3,7},{4,8},{5,9},{6,10},{7,11},{8,12},{9,13},{1... | collective-permute-start | bytes 835592 | tf_op jit(solution)/shard_map/ppermute | solution.py:28
  157.1 15.4 %collective-permute-start.23 = (bf16[128,1024]{1,0:T(8,128)(2,1)S(1)}, bf16[128,1024]{1,0:T(8,128)(2,1)S(1)}, u32[]{:S(2)}, u32[]{:S(2)}) collective-permute-start(bf16[128,1024]{1,0:T(8,128)(2,1)S(1)} %get-tuple-element.139), channel_id=1, source_target_pairs={{0,1},{1,2},{2,3},{3,0},{4,5},{5,6},{6,7},{7,4},{8,9},{9,10},{10,1... | collective-permute-start | bytes 786440 | tf_op jit(solution)/shard_map/ppermute | solution.py:28
  157.1 15.4 %collective-permute-start.22 = (bf16[128,1024]{1,0:T(8,128)(2,1)S(1)}, bf16[128,1024]{1,0:T(8,128)(2,1)S(1)}, u32[]{:S(2)}, u32[]{:S(2)}) collective-permute-start(bf16[128,1024]{1,0:T(8,128)(2,1)S(1)} %get-tuple-element.138), channel_id=1, source_target_pairs={{0,2},{1,3},{2,0},{3,1},{4,6},{5,7},{6,4},{7,5},{8,10},{9,11},{10,... | collective-permute-start | bytes 786440 | tf_op jit(solution)/shard_map/ppermute | solution.py:28
  173.1 10.5 %collective-permute-start.24 = (bf16[128,2048]{1,0:T(8,128)(2,1)S(1)}, bf16[128,2048]{1,0:T(8,128)(2,1)S(1)}, u32[]{:S(2)}, u32[]{:S(2)}) collective-permute-start(bf16[128,2048]{1,0:T(8,128)(2,1)S(1)} %get-tuple-element.140), channel_id=1, source_target_pairs={{16,0},{32,16},{48,32},{64,48},{80,64},{96,80},{112,96},{17,1},{33... | collective-permute-start | bytes 1572872 | tf_op jit(solution)/shard_map/ppermute | solution.py:465
  (12 other events, 129.5 us)
